TPU v7x, 256 devices: a whole 4x4x8 slice. The times are simulated.
256 devices in a mesh: row: 8 (over z), lm: 32 (over x, y, core).
Axes of the slice: x: 4, y: 4, z: 8, core: 2. Of those that a mesh axis runs over, the one named last changes fastest.
Arguments:
- fingerprints: int32 [4096, 2048], P('row'), may hold values from 0 to 7, as said below
- landmarks: int32 [16384, 2048], P('lm'), may hold values from 0 to 7, as said below
- whitening: bfloat16 [16384, 512], P('lm'), may hold values from -0.046875 to 0.046875
- memberships: int32 [4096], P('row'), may hold values from 0 to 4095
Outputs:
- centroids: float32 [4096, 512], P('row', 'lm')
Inputs may be any that keep to these rules, and one draw needn't show every extreme that they name: `fingerprints`: entries are counts; every row has at least one nonzero entry. `landmarks`: entries are counts; every row has at least one nonzero entry.
All inputs are finite; a program needn't handle non-finite values.
Results may differ from a plain program's by a relative error of at most 0.0025.
Values sent between devices are 32-bit elements; how exact they have to be, the bound alone decides.
No kernel may reach another device: no remote copies, remote signals or barrier semaphores. Data moves between devices by JAX's collectives and lax.ppermute only.
A program may use at most 64 MiB of HBM per device.

v0:
```python
import jax
import jax.numpy as jnp
from jax import lax
from jax.sharding import PartitionSpec as P

LEVELS = 7
CENT = 4096


def on_device(fingerprints, landmarks, whitening, memberships):
    shared = jnp.zeros((fingerprints.shape[0], landmarks.shape[0]), jnp.float32)
    for level in range(1, LEVELS + 1):
        left = (fingerprints >= level).astype(jnp.bfloat16)
        right = (landmarks >= level).astype(jnp.bfloat16)
        shared = shared + lax.dot_general(
            left, right, (((1,), (1,)), ((), ())), preferred_element_type=jnp.float32
        )
    row_total = jnp.sum(fingerprints, axis=1).astype(jnp.float32)
    land_total = jnp.sum(landmarks, axis=1).astype(jnp.float32)
    kernel = (shared / (row_total[:, None] + land_total[None, :] - shared)).astype(jnp.bfloat16)
    lm_count = lax.axis_size("lm")
    labels = jnp.arange(CENT, dtype=jnp.int32)
    onehot = (labels[:, None] == memberships[None, :]).astype(jnp.float32)
    counts_local = jnp.sum(onehot, axis=1)
    owned = kernel.shape[0] // lm_count
    raw = lax.psum_scatter(
        jnp.dot(kernel, whitening, preferred_element_type=jnp.float32),
        "lm",
        scatter_dimension=0,
        tiled=True,
    )
    features = raw / jnp.sqrt(jnp.mean(raw * raw, axis=1, keepdims=True) + 1e-06)
    member_block = lax.dynamic_slice_in_dim(onehot, lax.axis_index("lm") * owned, owned, 1)
    partial_value = jnp.dot(
        member_block, features, preferred_element_type=jnp.float32, precision=lax.Precision.HIGHEST
    )
    partial_value = lax.psum_scatter(partial_value, "lm", scatter_dimension=1, tiled=True)
    sums, counts = (
        lax.psum_scatter(partial_value, "row", scatter_dimension=0, tiled=True),
        lax.psum_scatter(counts_local, "row", scatter_dimension=0, tiled=True),
    )
    return sums / jnp.maximum(counts, 1.0)[:, None]


def solution(mesh):
    in_specs = (P("row", None), P("lm", None), P("lm", None), P("row"))
    out_specs = P("row", "lm")
    return jax.shard_map(
        on_device, mesh=mesh, in_specs=in_specs, out_specs=out_specs, check_vma=False
    )
```

profile of v0, /device:TPU:1, one launch (start us, length us, event | category | flops | bytes accessed | tf_op | source)
XLA Modules:
  0.0 276.0 jit_solution(16099025959104987612)
XLA Ops:
  6.5 5.9 %fusion.12 = f32[512,512]{1,0:T(8,128)} fusion(s32[512,2048]{1,0:T(8,128)} %param.5, s32[512,2048]{1,0:T(8,128)} %param.4), kind=kOutput, calls=%fused_computation.14 | convolution fusion | flops 1075838976 | bytes 9437184 | tf_op jit(solution)/shard_map/dot_general | solution.py:15
  12.5 2.4 fusion.15
  14.9 1.4 fusion.6
  16.3 1.4 fusion
  17.6 2.5 reduce_sum.36
  20.1 2.5 reduce_sum.37
  22.6 5.5 %fusion.35 = f32[512,512]{1,0:T(8,128)S(1)} fusion(f32[512,512]{1,0:T(8,128)} %fusion.12, f32[512,512]{1,0:T(8,128)} %fusion.15, s32[512,2048]{1,0:T(8,128)} %param.5, s32[512,2048]{1,0:T(8,128)} %param.4), kind=kOutput, calls=%fused_computation.34 | convolution fusion | flops 1076363264 | bytes 11534336 | tf_op jit(solution)/shard_map/dot_general | solution.py:15
  28.1 1.0 copy-done.4
  29.1 2.4 fusion.45
  31.5 6.4 %fusion.71 = f32[512,512]{1,0:T(8,128)} fusion(bf16[512,512]{1,0:T(8,128)(2,1)S(1)} %copy-done, f32[512,512]{1,0:T(8,128)S(1)} %fusion, f32[512,512]{1,0:T(8,128)} %fusion.45, s32[512,2048]{1,0:T(8,128)} %param.5, s32[512,2048]{1,0:T(8,128)} %param.4, f32[512]{0:T(512)S(1)} %convert_element_type.17, f32[512]{0:T(512)S(1)} %convert_element_type.16), kind=kOutput, calls=%fused_computation.40 | convolution fusion | flops 1345847296 | bytes 12062720 | tf_op jit(solution)/shard_map/dot_general | solution.py:27
  37.9 0.2 reduce-scatter.6.cloned.1.call-start
  38.2 1.7 iota_compare_fusion
  39.9 85.5 %reduce-scatter.4.cloned.1.call-done = f32[16,512]{1,0:T(8,128)} async-done(((f32[512,512]{1,0:T(8,128)}), f32[16,512]{1,0:T(8,128)}) %reduce-scatter.4.cloned.1.call-update) | async-done | bytes 32784 | tf_op jit(solution)/shard_map/reduce_scatter | solution.py:26
  125.4 0.9 multiply_reduce_fusion
  126.3 6.8 %fusion.28 = f32[4096,512]{0,1:T(8,128)} fusion(pred[4096,512]{1,0:T(32,128)(4,1)S(1)} %iota_compare_fusion, s32[]{:T(128)S(6)} %select_n.3, f32[16,512]{1,0:T(8,128)} %reduce-scatter.4.cloned.1.call-done, f32[16]{0:T(128)S(1)} %add_sqrt_fusion), kind=kOutput, calls=%fused_computation.30 | convolution fusion | flops 402661376 | bytes 8946180 | tf_op jit(solution)/shard_map/dot_general | solution.py:34
  133.1 0.0 reduce-scatter.6.cloned.1.call-update
  133.1 0.0 reduce-scatter.8.cloned.1.call-start
  133.1 99.8 %reduce-scatter.6.cloned.1.call-done = f32[4096,16]{0,1:T(8,128)} async-done(((f32[4096,512]{0,1:T(8,128)}), f32[4096,16]{0,1:T(8,128)}) %reduce-scatter.6.cloned.1.call-update) | async-done | bytes 262160 | tf_op jit(solution)/shard_map/reduce_scatter | solution.py:37
  233.0 0.6 dynamic-slice
  234.2 1.0 convert_reduce_fusion
  235.2 24.0 %all-reduce = f32[4096]{0:T(1024)S(1)} all-reduce(f32[4096]{0:T(1024)S(1)} %convert_reduce_fusion), channel_id=5, replica_groups=mesh['row'=8,'lm'=32] {'row'}, use_global_device_ids=true, to_apply=%region_7.0.clone | all-reduce | flops 4096 | bytes 32768
  259.2 0.1 dynamic-slice_maximum_fusion
  259.2 8.8 %reduce-scatter.8.cloned.1.call-done = f32[512,16]{0,1:T(8,128)} async-done(((f32[4096,16]{0,1:T(8,128)}), f32[512,16]{0,1:T(8,128)}) %reduce-scatter.8.cloned.1.call-update) | async-done | bytes 32784 | tf_op jit(solution)/shard_map/reduce_scatter | solution.py:39
  268.1 1.4 broadcast_divide_fusion
  (19 shorter events, 0.1 us)
Async XLA Ops:
  6.5 25.0 %copy-start = (bf16[512,512]{1,0:T(8,128)(2,1)S(1)}, bf16[512,512]{1,0:T(8,128)(2,1)}, u32[]{:S(2)}) copy-start(bf16[512,512]{1,0:T(8,128)(2,1)} %param.6) | copy-start | bytes 1572868
  6.5 118.9 %reduce-scatter.4.cloned.1.call-start = ((), (), s32[]{:S(2)}) async-start(), calls=%async_computation.3 | async-start | bytes 1081344 | tf_op jit(solution)/shard_map/reduce_scatter | solution.py:26
  6.5 6.0 %copy-start.1 = (s32[512,2048]{1,0:T(8,128)S(1)}, s32[512,2048]{1,0:T(8,128)}, u32[]{:S(2)}) copy-start(s32[512,2048]{1,0:T(8,128)} %param.5) | copy-start | bytes 12582916
  6.5 6.0 %copy-start.3 = (s32[512,2048]{1,0:T(8,128)S(1)}, s32[512,2048]{1,0:T(8,128)}, u32[]{:S(2)}) copy-start(s32[512,2048]{1,0:T(8,128)} %param.4) | copy-start | bytes 12582916
  22.6 5.5 %copy-start.2 = (s32[512,2048]{1,0:T(8,128)S(1)}, s32[512,2048]{1,0:T(8,128)}, u32[]{:S(2)}) copy-start(s32[512,2048]{1,0:T(8,128)} %param.5) | copy-start | bytes 12582916
  22.6 6.5 %copy-start.4 = (s32[512,2048]{1,0:T(8,128)S(1)}, s32[512,2048]{1,0:T(8,128)}, u32[]{:S(2)}) copy-start(s32[512,2048]{1,0:T(8,128)} %param.4) | copy-start | bytes 12582916
  31.5 6.6 %copy-start.5 = (s32[512]{0:T(512)S(1)}, s32[512]{0:T(512)}, u32[]{:S(2)}) copy-start(s32[512]{0:T(512)} %param.7) | copy-start | bytes 6148
  37.9 195.1 %reduce-scatter.6.cloned.1.call-start = ((), (), s32[]{:S(2)}) async-start(), calls=%async_computation.4 | async-start | bytes 8650752 | tf_op jit(solution)/shard_map/reduce_scatter | solution.py:37
  133.1 99.9 %copy-start.6 = (u32[256]{0:T(256)S(1)}, u32[256]{0:T(256)}, u32[]{:S(2)}) copy-start(u32[256]{0:T(256)} %constant.35) | copy-start | bytes 3076
  133.1 135.0 %reduce-scatter.8.cloned.1.call-start = ((), (), s32[]{:S(2)}) async-start(), calls=%async_computation.5 | async-start | bytes 294912 | tf_op jit(solution)/shard_map/reduce_scatter | solution.py:39
Sparse Core Ops, SparseCore 0:
  38.0 87.3 reduce-scatter.3
  133.2 99.7 reduce-scatter.5
  235.5 32.5 reduce-scatter.7
where the time goes:
time: 281 us; the launch traced here: 276 us
  waiting for transfers between devices  194 us (69%)
  matrix products  32.1 us (11%)
  blocking collectives  24 us (9%)
  between operations  13.9 us (5%)
  other arithmetic  9.94 us (4%)
    reduce_scatter x1, waiting for transfers between devices, on_device(): lax.psum_scatter(partial_value, 'lm', scatter_dimension=1, tiled=True)  99.8 us
    reduce_scatter x1, waiting for transfers between devices, on_device(): lax.psum_scatter(jnp.dot(kernel, whitening, preferred_element_type=jnp.fl...  85.5 us
    unnamed x1, blocking collectives  24 us
    dot_general x6, matrix products, on_device(): lax.dot_general(left, right, (((1,), (1,)), ((), ())), preferred_element_...  19 us
    reduce_scatter x1, waiting for transfers between devices, on_device(): lax.psum_scatter(partial_value, 'row', scatter_dimension=0, tiled=True)  8.83 us
    dot_general x1, matrix products, on_device(): jnp.dot(member_block, features, preferred_element_type=jnp.float32, preci...  6.79 us
    dot_general x1, matrix products, on_device(): jnp.dot(kernel, whitening, preferred_element_type=jnp.float32)  6.37 us
  transfers between devices with their start and end apart: 3, of which 3 were waited for; matrix products, arithmetic and copies ran while one was open for 1% of the time, Pallas kernels for 0%

commit v1 on v0

v1 whole, which is shorter than its diff:
```python
import functools

import jax
import jax.numpy as jnp
from jax import lax
from jax.experimental import pallas as pl
from jax.experimental.pallas import tpu as pltpu
from jax.sharding import PartitionSpec as P

LEVELS = 7
F8 = jnp.float8_e4m3fn
CHUNKS = (512, 512, 512, 512)
MIB = 1 << 20


def dot_nt(left, right):
    return lax.dot_general(left, right, (((1,), (1,)), ((), ())), preferred_element_type=jnp.float32)


def partial_features(half_ref, fp, lm, w, other, own, fp_v, lm_v, w_v, shared, row_total, land_total, sem):
    copies, at = [], 0
    for i, width in enumerate(CHUNKS):
        where = (slice(None), pl.ds(at, width))
        pair = (
            pltpu.make_async_copy(fp.at[where], fp_v.at[where], sem.at[2 * i]),
            pltpu.make_async_copy(lm.at[where], lm_v.at[where], sem.at[2 * i + 1]),
        )
        for copy in pair:
            copy.start()
        copies.append(pair)
        at += width
    w_copy = pltpu.make_async_copy(w, w_v, sem.at[2 * len(CHUNKS)])
    w_copy.start()
    one, zero = jnp.ones((), jnp.bfloat16), jnp.zeros((), jnp.bfloat16)
    at = 0
    for i, width in enumerate(CHUNKS):
        for copy in copies[i]:
            copy.wait()
        a = fp_v[:, at : at + width].astype(jnp.float32).astype(jnp.bfloat16)
        b = lm_v[:, at : at + width].astype(jnp.float32).astype(jnp.bfloat16)
        at += width
        rows = jnp.sum(a.astype(jnp.float32), axis=1, keepdims=True)
        lands = dot_nt(jnp.ones((8, width), jnp.bfloat16), b)[:1]
        left, right = [], []
        for level in range(1, LEVELS + 1):
            t = jnp.bfloat16(level)
            left.append((a if level == LEVELS else jnp.minimum(a, t)).astype(F8))
            right.append(jnp.where(b == t, one, zero).astype(F8))
        part = dot_nt(jnp.concatenate(left, 1), jnp.concatenate(right, 1))
        if i == 0:
            shared[...], row_total[...], land_total[...] = part, rows, lands
        else:
            shared[...] += part
            row_total[...] += rows
            land_total[...] += lands
    w_copy.wait()
    half = shared.shape[0] // 2
    mine = half_ref[0]
    for out, which in ((other, 1 - mine), (own, mine)):
        rows = pl.ds(pl.multiple_of(which * half, half), half)
        s = shared[rows, :]
        kernel = (s / (row_total[rows, :] + land_total[...] - s)).astype(jnp.bfloat16)
        out[...] = jnp.dot(kernel, w_v[...], preferred_element_type=jnp.float32)


def normalise(parts, out, turned):
    raw = parts[0]
    for i in range(1, parts.shape[0]):
        raw = raw + parts[i]
    rows, feat = raw.shape
    features = raw / jnp.sqrt(jnp.mean(raw * raw, axis=1, keepdims=True) + 1e-06)
    padded = jnp.concatenate([features, jnp.zeros((128 - rows, feat), jnp.float32)], 0)
    turned[...] = padded.T
    owners = feat // 16
    copies = out.shape[0] // (2 * owners)
    for h in range(2):
        block = jnp.concatenate(
            [turned[pl.ds(8 * h + f, owners, stride=16), :][:, :rows] for f in range(8)], 1
        )
        for z in range(copies):
            out[pl.ds(2 * owners * z + h, owners, stride=2), :] = block


def centroid_update(blocks, member, first_ref, out, *turned):
    sources, rows = member.shape
    cents = out.shape[1]
    for h in range(2):
        columns = blocks[pl.ds(h, sources, stride=2), :].T
        for part, ref in enumerate(turned):
            ref[pl.ds(128 * h, 128), :] = columns[:, 128 * part : 128 * (part + 1)]
    label = lax.broadcasted_iota(jnp.int32, (sources, cents), 1)
    local = member[...] - first_ref[0]
    acc = jnp.zeros((64, cents), jnp.float32)
    for j in range(rows):
        value = jnp.concatenate([ref[pl.ds(j, 16, stride=16), :] for ref in turned], 1)
        high = value.astype(jnp.bfloat16)
        rest = value - high.astype(jnp.float32)
        mid = rest.astype(jnp.bfloat16)
        low = (rest - mid.astype(jnp.float32)).astype(jnp.bfloat16)
        left = jnp.concatenate([high, mid, low, jnp.ones((16, sources), jnp.bfloat16)], 0)
        onehot = jnp.where(local[:, j : j + 1] == label, 1.0, 0.0).astype(jnp.bfloat16)
        acc = acc + jnp.dot(left, onehot, preferred_element_type=jnp.float32)
    sums = acc[0:16] + (acc[16:32] + acc[32:48])
    out[...] = sums / jnp.maximum(acc[48:49], 1.0)


def on_device(fingerprints, landmarks, whitening, memberships):
    rows, width = fingerprints.shape
    lands, feat = whitening.shape
    n_row, n_lm = lax.axis_size("row"), lax.axis_size("lm")
    chips = n_lm // 2
    owned = rows // n_lm
    half = rows // 2
    core = lax.axis_index("lm") % 2
    hbm, vmem, smem = (
        pl.BlockSpec(memory_space=m) for m in (pltpu.HBM, pltpu.VMEM, pltpu.SMEM)
    )
    other, own = pl.pallas_call(
        partial_features,
        in_specs=[smem, hbm, hbm, hbm],
        out_specs=[vmem, vmem],
        out_shape=[jax.ShapeDtypeStruct((half, feat), jnp.float32)] * 2,
        scratch_shapes=[
            pltpu.VMEM((rows, width), jnp.int32),
            pltpu.VMEM((lands, width), jnp.int32),
            pltpu.VMEM((lands, feat), jnp.bfloat16),
            pltpu.VMEM((rows, lands), jnp.float32),
            pltpu.VMEM((rows, 1), jnp.float32),
            pltpu.VMEM((1, lands), jnp.float32),
            pltpu.SemaphoreType.DMA((2 * len(CHUNKS) + 1,)),
        ],
        compiler_params=pltpu.CompilerParams(vmem_limit_bytes=60 * MIB),
        name="partial_features",
    )(core[None].astype(jnp.int32), fingerprints, landmarks, whitening)

    theirs = lax.ppermute(other, "lm", [(i, i ^ 1) for i in range(n_lm)])
    both = own + theirs
    parts = lax.all_to_all(
        both, "lm", 0, 0, tiled=True,
        axis_index_groups=[[2 * q + k for q in range(chips)] for k in range(2)],
    )

    spread = jnp.broadcast_to(memberships.reshape(1, -1, 128), (n_row, rows // 128, 128))
    member = lax.all_to_all(spread, "row", 0, 0, tiled=True)
    member = member.reshape(n_row, 2, chips, owned).transpose(0, 2, 1, 3).reshape(n_row * n_lm, owned)

    blocks = pl.pallas_call(
        normalise,
        in_specs=[vmem],
        out_specs=vmem,
        out_shape=jax.ShapeDtypeStruct((n_row * n_lm * 2, 128), jnp.float32),
        scratch_shapes=[pltpu.VMEM((feat, 128), jnp.float32)],
        name="normalise",
    )(parts.reshape(chips, owned, feat))
    blocks = lax.all_to_all(blocks, ("row", "lm"), 0, 0, tiled=True)

    cents = 4096 // n_row
    first = (lax.axis_index("row") * cents)[None].astype(jnp.int32)
    out = pl.pallas_call(
        centroid_update,
        in_specs=[vmem, vmem, smem],
        out_specs=vmem,
        out_shape=jax.ShapeDtypeStruct((feat // n_lm, cents), jnp.float32),
        scratch_shapes=[pltpu.VMEM((256, 128), jnp.float32)] * (n_row * n_lm // 128),
        name="centroid_update",
    )(blocks, member, first)
    return out.T


def solution(mesh):
    in_specs = (P("row", None), P("lm", None), P("lm", None), P("row"))
    out_specs = P("row", "lm")
    return jax.shard_map(
        on_device, mesh=mesh, in_specs=in_specs, out_specs=out_specs, check_vma=False
    )
```

time: 281 us -> 72 us (0.26); the launches traced: 276 us -> 71.7 us
  waiting for transfers between devices: 194 us -> 20.8 us
  matrix products: 32.1 us -> 0 us
  starting transfers between devices: 0.27 us -> 20 us
  between operations: 13.9 us -> 0.04 us
  Pallas kernels: 0 us -> 12.3 us
  other arithmetic: 9.94 us -> 1.12 us
  blocking collectives: 24 us -> 15.3 us
    reduce_scatter x3 -> x0, waiting for transfers between devices: 194 us -> none  [the longest x1 99.8 us: on_device(): lax.psum_scatter(partial_value, 'lm', scatter_dimension=1, tiled=True)]
    dot_general x8 -> x0, matrix products: 32.1 us -> none  [the longest x6 19 us: on_device(): lax.dot_general(left, right, (((1,), (1,)), ((), ())), preferred_element_...]
    unnamed x1 -> x0, blocking collectives: 24 us -> none
    all_to_all x0 -> x2, waiting for transfers between devices: none -> 19 us  [the longest x1 14.6 us: on_device(): blocks = lax.all_to_all(blocks, ('row', 'lm'), 0, 0, tiled=True)]
    all_to_all x0 -> x2, starting transfers between devices: none -> 16.7 us  [the longest x1 8.48 us: on_device(): blocks = lax.all_to_all(blocks, ('row', 'lm'), 0, 0, tiled=True)]
    all_to_all x0 -> x1, blocking collectives: none -> 15.3 us  [on_device(): lax.all_to_all(both, 'lm', 0, 0, tiled=True, axis_index_groups=[[2 * q +...]
    pallas_call x0 -> x3, Pallas kernels: none -> 12.3 us  [the longest x1 7.58 us: on_device(): pl.pallas_call(partial_features, in_specs=[smem, hbm, hbm, hbm], out_spec...]
    reduce_sum x4 -> x0, other arithmetic: 6.75 us -> none  [the longest x1 2.46 us: on_device(): row_total = jnp.sum(fingerprints, axis=1).astype(jnp.float32)]
  transfers between devices with their start and end apart: 3 -> 3, of which waited for: 3 -> 3; matrix products, arithmetic and copies ran while one was open for 1% -> 1% of each run, Pallas kernels for 0% -> 3%
where the time goes in v1:
time: 72 us; the launch traced here: 71.7 us
  waiting for transfers between devices  20.8 us (29%)
  starting transfers between devices  20 us (28%)
  blocking collectives  15.3 us (21%)
  Pallas kernels  12.3 us (17%)
  local copies, waits for them, and re-layouts  2.13 us (3%)
  other arithmetic  1.12 us (2%)
    all_to_all x1, blocking collectives, on_device(): lax.all_to_all(both, 'lm', 0, 0, tiled=True, axis_index_groups=[[2 * q +...  15.3 us
    all_to_all x1, waiting for transfers between devices, on_device(): blocks = lax.all_to_all(blocks, ('row', 'lm'), 0, 0, tiled=True)  14.6 us
    all_to_all x1, starting transfers between devices, on_device(): blocks = lax.all_to_all(blocks, ('row', 'lm'), 0, 0, tiled=True)  8.48 us
    all_to_all x1, starting transfers between devices, on_device(): member = lax.all_to_all(spread, 'row', 0, 0, tiled=True)  8.19 us
    pallas_call x1, Pallas kernels, on_device(): pl.pallas_call(partial_features, in_specs=[smem, hbm, hbm, hbm], out_spec...  7.58 us
    all_to_all x1, waiting for transfers between devices, on_device(): member = lax.all_to_all(spread, 'row', 0, 0, tiled=True)  4.47 us
    ppermute x1, starting transfers between devices, on_device(): theirs = lax.ppermute(other, 'lm', [(i, i ^ 1) for i in range(n_lm)])  3.33 us
    pallas_call x1, Pallas kernels, on_device(): pl.pallas_call(centroid_update, in_specs=[vmem, vmem, smem], out_specs=vm...  2.59 us
  transfers between devices with their start and end apart: 3, of which 3 were waited for; matrix products, arithmetic and copies ran while one was open for 1% of the time, Pallas kernels for 3%

profile of v1, /device:TPU:1, one launch (start us, length us, event | category | flops | bytes accessed | tf_op | source)
XLA Modules:
  0.0 71.7 jit_solution(76866064341338171)
XLA Ops:
  0.0 0.0 copy-start.1
  0.0 7.6 %partial_features.1 = (f32[256,512]{1,0:T(8,128)}, f32[256,512]{1,0:T(8,128)}) custom-call(s32[1]{0:T(128)} %bitcast.half_ref, s32[512,2048]{1,0:T(8,128)} %fp.1, s32[512,2048]{1,0:T(8,128)} %lm.1, bf16[512,512]{1,0:T(8,128)(2,1)} %w.1), custom_call_target="tpu_custom_call" | custom-call | tf_op jit(solution)/shard_map/partial_features/pallas_call | solution.py:118
  7.6 3.3 %collective-permute-start = (f32[256,512]{1,0:T(8,128)}, f32[256,512]{1,0:T(8,128)S(1)}, u32[]{:S(2)}, u32[]{:S(2)}) collective-permute-start(f32[256,512]{1,0:T(8,128)} %get-tuple-element.8), channel_id=1, source_target_pairs={{0,1},{1,0},{2,3},{3,2},{4,5},{5,4},{6,7},{7,6},{8,9},{9,8},{10,11... | collective-permute-start | bytes 1572872 | tf_op jit(solution)/shard_map/ppermute | solution.py:136
  10.9 1.7 %collective-permute-done = f32[256,512]{1,0:T(8,128)S(1)} collective-permute-done((f32[256,512]{1,0:T(8,128)}, f32[256,512]{1,0:T(8,128)S(1)}, u32[]{:S(2)}, u32[]{:S(2)}) %collective-permute-start) | collective-permute-done | bytes 524320 | tf_op jit(solution)/shard_map/ppermute | solution.py:136
  12.7 1.1 %add.8 = f32[256,512]{1,0:T(8,128)S(1)} add(f32[256,512]{1,0:T(8,128)} %get-tuple-element.7, f32[256,512]{1,0:T(8,128)S(1)} %collective-permute-done) | non-fusion elementwise | flops 131072 | bytes 1572864 | tf_op jit(solution)/shard_map/add | solution.py:137
  13.8 15.3 %all_to_all.25.parts = f32[16,16,512]{2,1,0:T(8,128)} all-to-all(f32[16,16,512]{2,1,0:T(8,128)S(1)} %bitcast.9), channel_id=1, replica_groups={{0,2,4,6,8,10,12,14,16,18,20,22,24,26,28,30},{1,3,5,7,9,11,13,15,17,19,..., dimensions={0} | all-to-all | bytes 1048576 | tf_op jit(solution)/shard_map/all_to_all | solution.py:138
  29.1 0.0 copy-done.1
  29.1 0.6 broadcast_in_dim.15
  29.7 8.2 %all-to-all-start.2 = ((s32[8,4,128]{2,1,0:T(4,128)}), s32[8,4,128]{2,1,0:T(4,128)S(1)}, u32[]{:S(2)}, u32[]{:S(2)}) async-start(s32[8,4,128]{2,1,0:T(4,128)} %broadcast_in_dim.15), calls=%async_computation.2 | async-start | bytes 32768 | tf_op jit(solution)/shard_map/all_to_all | solution.py:144
  37.9 2.2 %normalise.1 = f32[512,128]{1,0:T(8,128)} custom-call(f32[16,16,512]{2,1,0:T(8,128)} %all_to_all.25.parts), custom_call_target="tpu_custom_call" | custom-call | tf_op jit(solution)/shard_map/normalise/pallas_call | solution.py:147
  40.0 4.5 %all-to-all-done.2 = s32[8,4,128]{2,1,0:T(4,128)S(1)} async-done(((s32[8,4,128]{2,1,0:T(4,128)}), s32[8,4,128]{2,1,0:T(4,128)S(1)}, u32[]{:S(2)}, u32[]{:S(2)}) %all-to-all-start.2) | async-done | bytes 16416 | tf_op jit(solution)/shard_map/all_to_all | solution.py:144
  44.5 8.5 %all-to-all-start.1 = ((f32[256,2,128]{2,1,0:T(2,128)}), f32[256,2,128]{2,1,0:T(2,128)S(1)}, u32[]{:S(2)}, u32[]{:S(2)}) async-start(f32[256,2,128]{2,1,0:T(2,128)} %bitcast.10), calls=%async_computation.1 | async-start | bytes 524288 | tf_op jit(solution)/shard_map/all_to_all | solution.py:155
  53.0 0.1 reshape.14
  53.1 0.7 %copy.5 = s32[8,16,2,16]{3,2,1,0:T(2,128)} copy(s32[8,16,2,16]{3,1,2,0:T(8,128)S(1)} %bitcast.12) | data formatting | bytes 32768 | tf_op jit(solution)/shard_map/transpose | solution.py:145
  53.8 14.6 %all-to-all-done.1 = f32[256,2,128]{2,1,0:T(2,128)S(1)} async-done(((f32[256,2,128]{2,1,0:T(2,128)}), f32[256,2,128]{2,1,0:T(2,128)S(1)}, u32[]{:S(2)}, u32[]{:S(2)}) %all-to-all-start.1) | async-done | bytes 262176 | tf_op jit(solution)/shard_map/all_to_all | solution.py:155
  68.4 0.0 copy-start
  68.4 0.7 copy-done
  69.1 2.6 %centroid_update.1 = f32[16,512]{1,0:T(8,128)} custom-call(f32[512,128]{1,0:T(8,128)} %bitcast.11, s32[256,16]{1,0:T(8,128)} %bitcast.13, s32[1]{0:T(128)} %bitcast.7.first_ref), custom_call_target="tpu_custom_call" | custom-call | tf_op jit(solution)/shard_map/centroid_update/pallas_call | solution.py:159
Async XLA Ops:
  0.0 29.1 %copy-start.1 = (s32[512]{0:T(512)S(1)}, s32[512]{0:T(512)}, u32[]{:S(2)}) copy-start(s32[512]{0:T(512)} %param.7) | copy-start | bytes 6148
  7.6 5.1 %collective-permute-start = (f32[256,512]{1,0:T(8,128)}, f32[256,512]{1,0:T(8,128)S(1)}, u32[]{:S(2)}, u32[]{:S(2)}) collective-permute-start(f32[256,512]{1,0:T(8,128)} %get-tuple-element.8), channel_id=1, source_target_pairs={{0,1},{1,0},{2,3},{3,2},{4,5},{5,4},{6,7},{7,6},{8,9},{9,8},{10,11... | collective-permute-start | bytes 1572872 | tf_op jit(solution)/shard_map/ppermute | solution.py:136
  29.7 14.8 %all-to-all-start.2 = ((s32[8,4,128]{2,1,0:T(4,128)}), s32[8,4,128]{2,1,0:T(4,128)S(1)}, u32[]{:S(2)}, u32[]{:S(2)}) async-start(s32[8,4,128]{2,1,0:T(4,128)} %broadcast_in_dim.15), calls=%async_computation.2 | async-start | bytes 32768 | tf_op jit(solution)/shard_map/all_to_all | solution.py:144
  44.5 23.9 %all-to-all-start.1 = ((f32[256,2,128]{2,1,0:T(2,128)}), f32[256,2,128]{2,1,0:T(2,128)S(1)}, u32[]{:S(2)}, u32[]{:S(2)}) async-start(f32[256,2,128]{2,1,0:T(2,128)} %bitcast.10), calls=%async_computation.1 | async-start | bytes 524288 | tf_op jit(solution)/shard_map/all_to_all | solution.py:155
  68.4 0.7 copy-start

commit v2 on v1

v2 whole, which is shorter than its diff:
```python
import jax
import jax.numpy as jnp
from jax import lax
from jax.experimental import pallas as pl
from jax.experimental.pallas import tpu as pltpu
from jax.sharding import Mesh
from jax.sharding import PartitionSpec as P

LEVELS = 7
F8 = jnp.float8_e4m3fn
CHUNKS = (128, 128, 256, 512, 512, 512)
MIB = 1 << 20


def dot_nt(left, right):
    return lax.dot_general(left, right, (((1,), (1,)), ((), ())), preferred_element_type=jnp.float32)


def partial_features(half_ref, fp, lm, w, other, own, fp_v, lm_v, w_v, shared, row_total, land_total, *rest):
    factors, sem = (rest[0:2], rest[2:4]), rest[4]
    copies, starts, at = [], [], 0
    for i, width in enumerate(CHUNKS):
        where = (slice(None), pl.ds(at, width))
        pair = (
            pltpu.make_async_copy(fp.at[where], fp_v.at[where], sem.at[2 * i]),
            pltpu.make_async_copy(lm.at[where], lm_v.at[where], sem.at[2 * i + 1]),
        )
        for copy in pair:
            copy.start()
        copies.append(pair)
        starts.append(at)
        at += width
    w_copy = pltpu.make_async_copy(w, w_v, sem.at[2 * len(CHUNKS)])
    w_copy.start()
    one, zero = jnp.ones((), jnp.bfloat16), jnp.zeros((), jnp.bfloat16)

    def convert(i):
        width, (left, right) = CHUNKS[i], factors[i % 2]
        for copy in copies[i]:
            copy.wait()
        a = fp_v[:, starts[i] : starts[i] + width].astype(jnp.float32)
        b = lm_v[:, starts[i] : starts[i] + width].astype(jnp.float32).astype(jnp.bfloat16)
        rows = jnp.sum(a, axis=1, keepdims=True)
        lands = dot_nt(jnp.ones((8, width), jnp.bfloat16), b)[:1]
        if i == 0:
            row_total[...], land_total[...] = rows, lands
        else:
            row_total[...] += rows
            land_total[...] += lands
        a = a.astype(jnp.bfloat16)
        for level in range(1, LEVELS + 1):
            t = jnp.bfloat16(level)
            where = slice((level - 1) * width, level * width)
            left[:, where] = (a if level == LEVELS else jnp.minimum(a, t)).astype(F8)
            right[:, where] = jnp.where(b == t, one, zero).astype(F8)

    convert(0)
    for i, width in enumerate(CHUNKS):
        left, right = factors[i % 2]
        part = dot_nt(left[:, : LEVELS * width], right[:, : LEVELS * width])
        if i == 0:
            shared[...] = part
        else:
            shared[...] += part
        if i + 1 < len(CHUNKS):
            convert(i + 1)
    w_copy.wait()
    half = shared.shape[0] // 2
    mine = half_ref[0]
    for which in (1 - mine, mine):
        rows = pl.ds(pl.multiple_of(which * half, half), half)
        s = shared[rows, :]
        kernel = (s / (row_total[rows, :] + land_total[...] - s)).astype(jnp.bfloat16)
        out = own if which is mine else other
        out[...] = jnp.dot(kernel, w_v[...], preferred_element_type=jnp.float32)


def add_theirs(own, theirs, both):
    both[...] = own[...] + theirs[...]


def normalise(place_ref, parts, member, out, turned):
    raw = parts[0]
    for i in range(1, parts.shape[0]):
        raw = raw + parts[i]
    rows, feat = raw.shape
    features = raw / jnp.sqrt(jnp.mean(raw * raw, axis=1, keepdims=True) + 1e-06)
    padded = jnp.concatenate([features, jnp.zeros((128 - rows, feat), jnp.float32)], 0)
    turned[...] = padded.T
    owners = feat // 16
    copies = out.shape[0] // (3 * owners)
    line = member[pl.ds(place_ref[0], 1), :].astype(jnp.float32)
    line = pltpu.roll(line, 128 - rows * place_ref[1], axis=1)
    line = jnp.broadcast_to(line, (owners, 128))
    for h in range(3):
        block = line
        if h < 2:
            block = jnp.concatenate(
                [turned[pl.ds(8 * h + f, owners, stride=16), :][:, :rows] for f in range(8)], 1
            )
        for z in range(copies):
            out[pl.ds(3 * owners * z + h, owners, stride=3), :] = block


def centroid_update(blocks, first_ref, out, *turned):
    sources, rows, cents = blocks.shape[0] // 3, 16, out.shape[1]
    for h in range(2):
        columns = blocks[pl.ds(h, sources, stride=3), :].T
        for part, ref in enumerate(turned):
            ref[pl.ds(128 * h, 128), :] = columns[:, 128 * part : 128 * (part + 1)]
    label = lax.broadcasted_iota(jnp.int32, (sources, cents), 1)
    local = blocks[pl.ds(2, sources, stride=3), :].astype(jnp.int32) - first_ref[0]
    acc = jnp.zeros((64, cents), jnp.float32)
    for j in range(rows):
        value = jnp.concatenate([ref[pl.ds(j, 16, stride=16), :] for ref in turned], 1)
        high = value.astype(jnp.bfloat16)
        rest = value - high.astype(jnp.float32)
        mid = rest.astype(jnp.bfloat16)
        low = (rest - mid.astype(jnp.float32)).astype(jnp.bfloat16)
        left = jnp.concatenate([high, mid, low, jnp.ones((16, sources), jnp.bfloat16)], 0)
        onehot = jnp.where(local[:, j : j + 1] == label, 1.0, 0.0).astype(jnp.bfloat16)
        acc = acc + jnp.dot(left, onehot, preferred_element_type=jnp.float32)
    sums = acc[0:16] + (acc[16:32] + acc[32:48])
    out[...] = sums / jnp.maximum(acc[48:49], 1.0)


def on_device(fingerprints, landmarks, whitening, memberships):
    rows, width = fingerprints.shape
    lands, feat = whitening.shape
    n_row, chips, cores = (lax.axis_size(a) for a in ("row", "chip", "core"))
    n_lm = chips * cores
    owned = rows // n_lm
    half = rows // 2
    core = lax.axis_index("core").astype(jnp.int32)
    hbm, vmem, smem = (
        pl.BlockSpec(memory_space=m) for m in (pltpu.HBM, pltpu.VMEM, pltpu.SMEM)
    )
    factor = pltpu.VMEM((rows, LEVELS * max(CHUNKS)), F8)
    small = pltpu.CompilerParams(vmem_limit_bytes=12 * MIB)
    other, own = pl.pallas_call(
        partial_features,
        in_specs=[smem, hbm, hbm, hbm],
        out_specs=[vmem, vmem],
        out_shape=[jax.ShapeDtypeStruct((half, feat), jnp.float32)] * 2,
        scratch_shapes=[
            pltpu.VMEM((rows, width), jnp.int32),
            pltpu.VMEM((lands, width), jnp.int32),
            pltpu.VMEM((lands, feat), jnp.bfloat16),
            pltpu.VMEM((rows, lands), jnp.float32),
            pltpu.VMEM((rows, 1), jnp.float32),
            pltpu.VMEM((1, lands), jnp.float32),
            factor, factor, factor, factor,
            pltpu.SemaphoreType.DMA((2 * len(CHUNKS) + 1,)),
        ],
        compiler_params=pltpu.CompilerParams(vmem_limit_bytes=57 * MIB),
        name="partial_features",
    )(core[None], fingerprints, landmarks, whitening)

    theirs = lax.ppermute(other, "core", [(0, 1), (1, 0)])
    both = pl.pallas_call(
        add_theirs,
        in_specs=[vmem] * 2,
        out_specs=vmem,
        out_shape=jax.ShapeDtypeStruct((half, feat), jnp.float32),
        compiler_params=small,
        name="add_theirs",
    )(own, theirs)
    parts = lax.all_to_all(both, "chip", 0, 0, tiled=True)

    chip = lax.axis_index("chip").astype(jnp.int32)
    each = 128 // owned
    place = jnp.stack([core * (half // 128) + chip // each, chip % each])
    blocks = pl.pallas_call(
        normalise,
        in_specs=[smem, vmem, vmem],
        out_specs=vmem,
        out_shape=jax.ShapeDtypeStruct((n_row * n_lm * 3, 128), jnp.float32),
        scratch_shapes=[pltpu.VMEM((feat, 128), jnp.float32)],
        compiler_params=small,
        name="normalise",
    )(place, parts.reshape(chips, owned, feat), memberships.reshape(-1, 128))
    blocks = lax.all_to_all(
        blocks.reshape(n_row * n_lm, 1, 3 * 128), ("row", "chip", "core"), 0, 0, tiled=True
    ).reshape(-1, 128)

    cents = 4096 // n_row
    first = (lax.axis_index("row") * cents)[None].astype(jnp.int32)
    out = pl.pallas_call(
        centroid_update,
        in_specs=[vmem, smem],
        out_specs=vmem,
        out_shape=jax.ShapeDtypeStruct((feat // n_lm, cents), jnp.float32),
        scratch_shapes=[pltpu.VMEM((256, 128), jnp.float32)] * (n_row * n_lm // 128),
        compiler_params=small,
        name="centroid_update",
    )(blocks, first)
    return out.T


def solution(mesh):
    lm = ("chip", "core")
    inner = Mesh(mesh.devices.reshape(mesh.shape["row"], -1, 2), ("row",) + lm)
    in_specs = (P("row", None), P(lm, None), P(lm, None), P("row"))
    out_specs = P("row", lm)
    return jax.shard_map(
        on_device, mesh=inner, in_specs=in_specs, out_specs=out_specs, check_vma=False
    )
```

time: 72 us -> 63 us (0.88)
  blocking collectives: 15.3 us -> 0 us
  waiting for transfers between devices: 20.8 us -> 29.1 us
  local copies, waits for them, and re-layouts: 2.13 us -> 1.04 us
  other arithmetic: 1.12 us -> 0.08 us
  starting transfers between devices: 20 us -> 21 us
  Pallas kernels: 12.3 us -> 11.4 us
    all_to_all x1 -> x0, blocking collectives: 15.3 us -> none  [on_device(): lax.all_to_all(both, 'lm', 0, 0, tiled=True, axis_index_groups=[[2 * q +...]
    all_to_all x2, waiting for transfers between devices: 19 us -> 27.4 us  [the longest x1 17.1 us: on_device(): lax.all_to_all(blocks.reshape(n_row * n_lm, 1, 3 * 128), ('row', 'chip',...]
    add x1 -> x0, other arithmetic: 1.12 us -> none  [on_device(): both = own + theirs]
    all_to_all x2, starting transfers between devices: 16.7 us -> 17.7 us  [the longest x1 12.7 us: on_device(): lax.all_to_all(blocks.reshape(n_row * n_lm, 1, 3 * 128), ('row', 'chip',...]
    pallas_call x2 -> x3, Pallas kernels: 4.75 us -> 4.15 us  [the longest x1 1.7 us: on_device(): pl.pallas_call(normalise, in_specs=[smem, vmem, vmem], out_specs=vmem, ou...]
  transfers between devices with their start and end apart: 3 -> 3, of which waited for: 3 -> 3; matrix products, arithmetic and copies ran while one was open for 1% -> 0% of each run, Pallas kernels for 3% -> 0%
where the time goes in v2:
time: 63 us; the launch traced here: 62.7 us
  waiting for transfers between devices  29.1 us (46%)
  starting transfers between devices  21 us (33%)
  Pallas kernels  11.4 us (18%)
  local copies, waits for them, and re-layouts  1.04 us (2%)
    all_to_all x1, waiting for transfers between devices, on_device(): lax.all_to_all(blocks.reshape(n_row * n_lm, 1, 3 * 128), ('row', 'chip',...  17.1 us
    all_to_all x1, starting transfers between devices, on_device(): lax.all_to_all(blocks.reshape(n_row * n_lm, 1, 3 * 128), ('row', 'chip',...  12.7 us
    all_to_all x1, waiting for transfers between devices, on_device(): parts = lax.all_to_all(both, 'chip', 0, 0, tiled=True)  10.3 us
    pallas_call x1, Pallas kernels, on_device(): pl.pallas_call(partial_features, in_specs=[smem, hbm, hbm, hbm], out_spec...  7.27 us
    all_to_all x1, starting transfers between devices, on_device(): parts = lax.all_to_all(both, 'chip', 0, 0, tiled=True)  5.02 us
    ppermute x1, starting transfers between devices, on_device(): theirs = lax.ppermute(other, 'core', [(0, 1), (1, 0)])  3.33 us
    ppermute x1, waiting for transfers between devices, on_device(): theirs = lax.ppermute(other, 'core', [(0, 1), (1, 0)])  1.75 us
    pallas_call x1, Pallas kernels, on_device(): pl.pallas_call(normalise, in_specs=[smem, vmem, vmem], out_specs=vmem, ou...  1.7 us
  transfers between devices with their start and end apart: 3, of which 3 were waited for; matrix products, arithmetic and copies ran while one was open for 0% of the time, Pallas kernels for 0%

profile of v2, /device:TPU:1, one launch (start us, length us, event | category | flops | bytes accessed | tf_op | source)
XLA Modules:
  0.0 62.7 jit_solution(14705912189423908038)
XLA Ops:
  0.0 0.0 copy-start.1
  0.0 7.3 %partial_features.1 = (f32[256,512]{1,0:T(8,128)}, f32[256,512]{1,0:T(8,128)}) custom-call(s32[1]{0:T(128)} %bitcast.2.half_ref, s32[512,2048]{1,0:T(8,128)} %fp.1, s32[512,2048]{1,0:T(8,128)} %lm.1, bf16[512,512]{1,0:T(8,128)(2,1)} %w.1), custom_call_target="tpu_custom_call" | custom-call | tf_op jit(solution)/shard_map/partial_features/pallas_call | solution.py:140
  7.3 3.3 %collective-permute-start = (f32[256,512]{1,0:T(8,128)}, f32[256,512]{1,0:T(8,128)S(1)}, u32[]{:S(2)}, u32[]{:S(2)}) collective-permute-start(f32[256,512]{1,0:T(8,128)} %get-tuple-element.8), channel_id=1, source_target_pairs={{0,1},{1,0},{2,3},{3,2},{4,5},{5,4},{6,7},{7,6},{8,9},{9,8},{10,11... | collective-permute-start | bytes 1572872 | tf_op jit(solution)/shard_map/ppermute | solution.py:159
  10.6 1.7 %collective-permute-done.theirs = f32[256,512]{1,0:T(8,128)S(1)} collective-permute-done((f32[256,512]{1,0:T(8,128)}, f32[256,512]{1,0:T(8,128)S(1)}, u32[]{:S(2)}, u32[]{:S(2)}) %collective-permute-start) | collective-permute-done | bytes 524320 | tf_op jit(solution)/shard_map/ppermute | solution.py:159
  12.4 0.0 copy-start
  12.4 1.0 %copy-done = f32[256,512]{1,0:T(8,128)S(1)} copy-done((f32[256,512]{1,0:T(8,128)S(1)}, f32[256,512]{1,0:T(8,128)}, u32[]{:S(2)}) %copy-start) | copy-done | bytes 524312
  13.4 0.8 %add_theirs.1 = f32[256,512]{1,0:T(8,128)} custom-call(f32[256,512]{1,0:T(8,128)S(1)} %copy-done, f32[256,512]{1,0:T(8,128)S(1)} %collective-permute-done.theirs), custom_call_target="tpu_custom_call" | custom-call | tf_op jit(solution)/shard_map/add_theirs/pallas_call | solution.py:160
  14.2 5.0 %all-to-all-start = ((f32[16,16,512]{2,1,0:T(8,128)}), f32[16,16,512]{2,1,0:T(8,128)S(1)}, u32[]{:S(2)}, u32[]{:S(2)}) async-start(f32[16,16,512]{2,1,0:T(8,128)} %bitcast.3), calls=%async_computation | async-start | bytes 1048576 | tf_op jit(solution)/shard_map/all_to_all | solution.py:168
  19.3 0.1 pad_add_fusion.place_ref
  19.4 10.3 %all-to-all-done.parts = f32[16,16,512]{2,1,0:T(8,128)S(1)} async-done(((f32[16,16,512]{2,1,0:T(8,128)}), f32[16,16,512]{2,1,0:T(8,128)S(1)}, u32[]{:S(2)}, u32[]{:S(2)}) %all-to-all-start) | async-done | bytes 524320 | tf_op jit(solution)/shard_map/all_to_all | solution.py:168
  29.6 0.0 copy-done.1
  29.6 1.7 %normalise.1 = f32[768,128]{1,0:T(8,128)} custom-call(s32[2]{0:T(128)S(1)} %pad_add_fusion.place_ref, f32[16,16,512]{2,1,0:T(8,128)S(1)} %all-to-all-done.parts, s32[4,128]{1,0:T(4,128)S(1)} %bitcast.10), custom_call_target="tpu_custom_call" | custom-call | tf_op jit(solution)/shard_map/normalise/pallas_call | solution.py:173
  31.3 12.7 %all-to-all-start.1 = ((f32[256,1,384]{2,1,0:T(1,128)}), f32[256,1,384]{2,1,0:T(1,128)S(1)}, u32[]{:S(2)}, u32[]{:S(2)}) async-start(f32[256,1,384]{2,1,0:T(1,128)} %bitcast.5), calls=%async_computation.1 | async-start | bytes 786432 | tf_op jit(solution)/shard_map/all_to_all | solution.py:182
  44.0 17.1 %all-to-all-done.1 = f32[256,1,384]{2,1,0:T(1,128)S(1)} async-done(((f32[256,1,384]{2,1,0:T(1,128)}), f32[256,1,384]{2,1,0:T(1,128)S(1)}, u32[]{:S(2)}, u32[]{:S(2)}) %all-to-all-start.1) | async-done | bytes 393248 | tf_op jit(solution)/shard_map/all_to_all | solution.py:182
  61.1 1.6 %centroid_update.1 = f32[16,512]{1,0:T(8,128)} custom-call(f32[768,128]{1,0:T(8,128)S(1)} %bitcast.9, s32[1]{0:T(128)} %bitcast.7.first_ref), custom_call_target="tpu_custom_call" | custom-call | tf_op jit(solution)/shard_map/centroid_update/pallas_call | solution.py:188
Async XLA Ops:
  0.0 29.6 %copy-start.1 = (s32[512]{0:T(512)S(1)}, s32[512]{0:T(512)}, u32[]{:S(2)}) copy-start(s32[512]{0:T(512)} %param.7) | copy-start | bytes 6148
  7.3 5.1 %collective-permute-start = (f32[256,512]{1,0:T(8,128)}, f32[256,512]{1,0:T(8,128)S(1)}, u32[]{:S(2)}, u32[]{:S(2)}) collective-permute-start(f32[256,512]{1,0:T(8,128)} %get-tuple-element.8), channel_id=1, source_target_pairs={{0,1},{1,0},{2,3},{3,2},{4,5},{5,4},{6,7},{7,6},{8,9},{9,8},{10,11... | collective-permute-start | bytes 1572872 | tf_op jit(solution)/shard_map/ppermute | solution.py:159
  12.4 1.0 %copy-start = (f32[256,512]{1,0:T(8,128)S(1)}, f32[256,512]{1,0:T(8,128)}, u32[]{:S(2)}) copy-start(f32[256,512]{1,0:T(8,128)} %get-tuple-element.7.own) | copy-start | bytes 1572868
  14.2 15.4 %all-to-all-start = ((f32[16,16,512]{2,1,0:T(8,128)}), f32[16,16,512]{2,1,0:T(8,128)S(1)}, u32[]{:S(2)}, u32[]{:S(2)}) async-start(f32[16,16,512]{2,1,0:T(8,128)} %bitcast.3), calls=%async_computation | async-start | bytes 1048576 | tf_op jit(solution)/shard_map/all_to_all | solution.py:168
  31.3 29.8 %all-to-all-start.1 = ((f32[256,1,384]{2,1,0:T(1,128)}), f32[256,1,384]{2,1,0:T(1,128)S(1)}, u32[]{:S(2)}, u32[]{:S(2)}) async-start(f32[256,1,384]{2,1,0:T(1,128)} %bitcast.5), calls=%async_computation.1 | async-start | bytes 786432 | tf_op jit(solution)/shard_map/all_to_all | solution.py:182

commit v3 on v2

v3 whole, which is shorter than its diff:
```python
import functools

import jax
import jax.numpy as jnp
from jax import lax
from jax.experimental import pallas as pl
from jax.experimental.pallas import tpu as pltpu
from jax.sharding import Mesh
from jax.sharding import PartitionSpec as P

LEVELS = 7
F8 = jnp.float8_e4m3fn
CHUNKS = (128, 128, 256, 512, 512, 512)
MIB = 1 << 20


def dot_nt(left, right):
    return lax.dot_general(left, right, (((1,), (1,)), ((), ())), preferred_element_type=jnp.float32)


def partial_features(fp, lm, w, other, own, fp_v, lm_v, w_v, turned_w, shared, row_total, land_total, *rest):
    factors, sem = (rest[0:2], rest[2:4]), rest[4]
    w_copy = pltpu.make_async_copy(w, w_v, sem.at[2 * len(CHUNKS)])
    w_copy.start()
    copies, starts, at = [], [], 0
    for i, width in enumerate(CHUNKS):
        where = (slice(None), pl.ds(at, width))
        pair = (
            pltpu.make_async_copy(fp.at[where], fp_v.at[where], sem.at[2 * i]),
            pltpu.make_async_copy(lm.at[where], lm_v.at[where], sem.at[2 * i + 1]),
        )
        for copy in pair:
            copy.start()
        copies.append(pair)
        starts.append(at)
        at += width
    one, zero = jnp.ones((), jnp.bfloat16), jnp.zeros((), jnp.bfloat16)

    feat = w_v.shape[1]
    half = feat // 2
    column = lax.broadcasted_iota(jnp.int32, (feat, half), 0)
    place = lax.broadcasted_iota(jnp.int32, (feat, half), 1)
    place = 2 * (place - place % 16) + place % 16
    this = lax.axis_index("core")
    w_copy.wait()
    for part, core in enumerate((1 - this, this)):
        pick = jnp.where(column == place + 16 * core, 1.0, 0.0).astype(jnp.bfloat16)
        picked = jnp.dot(w_v[...], pick, preferred_element_type=jnp.float32)
        turned_w[:, part * half : (part + 1) * half] = picked.astype(jnp.bfloat16)

    def convert(i):
        width, (left, right) = CHUNKS[i], factors[i % 2]
        for copy in copies[i]:
            copy.wait()
        a = fp_v[:, starts[i] : starts[i] + width].astype(jnp.float32)
        b = lm_v[:, starts[i] : starts[i] + width].astype(jnp.float32).astype(jnp.bfloat16)
        rows = jnp.sum(a, axis=1, keepdims=True)
        lands = dot_nt(jnp.ones((8, width), jnp.bfloat16), b)[:1]
        if i == 0:
            row_total[...], land_total[...] = rows, lands
        else:
            row_total[...] += rows
            land_total[...] += lands
        a = a.astype(jnp.bfloat16)
        for level in range(1, LEVELS + 1):
            t = jnp.bfloat16(level)
            where = slice((level - 1) * width, level * width)
            left[:, where] = (a if level == LEVELS else jnp.minimum(a, t)).astype(F8)
            right[:, where] = jnp.where(b == t, one, zero).astype(F8)

    convert(0)
    for i, width in enumerate(CHUNKS):
        left, right = factors[i % 2]
        part = dot_nt(left[:, : LEVELS * width], right[:, : LEVELS * width])
        if i == 0:
            shared[...] = part
        else:
            shared[...] += part
        if i + 1 < len(CHUNKS):
            convert(i + 1)
    step = 256
    for at in range(0, shared.shape[0], step):
        rows = pl.ds(at, step)
        s = shared[rows, :]
        kernel = (s / (row_total[rows, :] + land_total[...] - s)).astype(jnp.bfloat16)
        raw = jnp.dot(kernel, turned_w[...], preferred_element_type=jnp.float32)
        other[rows, :], own[rows, :] = raw[:, :half], raw[:, half:]


def add_theirs(own, theirs, both):
    both[...] = own[...] + theirs[...]


def sum_parts(parts, turned, squares):
    raw = parts[0]
    for i in range(1, parts.shape[0]):
        raw = raw + parts[i]
    rows, half = raw.shape
    raw = jnp.concatenate([raw, jnp.zeros((128 - rows, half), jnp.float32)], 0).T
    turned[...] = raw
    squares[...] = jnp.broadcast_to(jnp.sum(raw * raw, axis=0, keepdims=True), squares.shape)


def lay_out(turned, member, lines):
    owners = turned.shape[0] // 16
    rows, count = 128 // 4, lines.shape[0] - 1
    for h in range(count):
        lines[h] = jnp.concatenate(
            [turned[pl.ds(4 * h + f, owners, stride=16), :][:, :rows] for f in range(4)], 1
        )
    chip = lax.axis_index("chip")
    line = member[pl.ds(chip // 4, 1), :].astype(jnp.float32)
    line = pltpu.roll(line, 128 - rows * (chip % 4), axis=1)
    lines[count] = jnp.broadcast_to(line, (owners, 128))


def normalise(lines, mine, theirs, out, *, feat):
    count, owners, _ = lines.shape
    rows = 128 // 4
    root = jnp.sqrt((mine[...] + theirs[...])[:1] / feat + 1e-06)
    root = jnp.concatenate([root[:, :rows]] * 4, 1)
    for h in range(count):
        line = lines[h] / root if h + 1 < count else lines[h]
        for z in range(out.shape[0] // (count * owners)):
            out[pl.ds(count * owners * z + h, owners, stride=count), :] = line


def centroid_update(blocks, out, turned):
    count, rows, cents = 5, 32, out.shape[1]
    sources = blocks.shape[0] // count
    for h in range(count - 1):
        turned[pl.ds(128 * h, 128), :] = blocks[pl.ds(h, sources, stride=count), :].T
    label = lax.broadcasted_iota(jnp.int32, (sources, cents), 1)
    local = blocks[pl.ds(count - 1, sources, stride=count), :].astype(jnp.int32) - lax.axis_index("row") * cents
    acc = jnp.zeros((64, cents), jnp.float32)
    for j in range(0, rows, 2):
        both = (j, j + 1)
        value = jnp.concatenate([turned[pl.ds(i, 16, stride=rows), :] for i in both], 1)
        high = value.astype(jnp.bfloat16)
        rest = value - high.astype(jnp.float32)
        mid = rest.astype(jnp.bfloat16)
        low = (rest - mid.astype(jnp.float32)).astype(jnp.bfloat16)
        left = jnp.concatenate([high, mid, low, jnp.ones((16, 2 * sources), jnp.bfloat16)], 0)
        onehot = jnp.concatenate(
            [jnp.where(local[:, i : i + 1] == label, 1.0, 0.0).astype(jnp.bfloat16) for i in both], 0
        )
        acc = acc + jnp.dot(left, onehot, preferred_element_type=jnp.float32)
    sums = acc[0:16] + (acc[16:32] + acc[32:48])
    out[...] = sums / jnp.maximum(acc[48:49], 1.0)


def on_device(fingerprints, landmarks, whitening, memberships):
    rows, width = fingerprints.shape
    lands, feat = whitening.shape
    n_row, chips, cores = (lax.axis_size(a) for a in ("row", "chip", "core"))
    half = feat // cores
    owned = rows // chips
    sources, lines = n_row * chips, 5
    hbm, vmem = (pl.BlockSpec(memory_space=m) for m in (pltpu.HBM, pltpu.VMEM))
    factor = pltpu.VMEM((rows, LEVELS * max(CHUNKS)), F8)
    small = pltpu.CompilerParams(vmem_limit_bytes=12 * MIB)

    def f32(*shape):
        return jax.ShapeDtypeStruct(shape, jnp.float32)

    other, own = pl.pallas_call(
        partial_features,
        in_specs=[hbm] * 3,
        out_specs=[vmem, vmem],
        out_shape=[f32(rows, half)] * 2,
        scratch_shapes=[
            pltpu.VMEM((rows, width), jnp.int32),
            pltpu.VMEM((lands, width), jnp.int32),
            pltpu.VMEM((lands, feat), jnp.bfloat16),
            pltpu.VMEM((lands, feat), jnp.bfloat16),
            pltpu.VMEM((rows, lands), jnp.float32),
            pltpu.VMEM((rows, 1), jnp.float32),
            pltpu.VMEM((1, lands), jnp.float32),
            factor, factor, factor, factor,
            pltpu.SemaphoreType.DMA((2 * len(CHUNKS) + 1,)),
        ],
        compiler_params=pltpu.CompilerParams(vmem_limit_bytes=40 * MIB),
        name="partial_features",
    )(
        *(pltpu.with_memory_space_constraint(x, pltpu.HBM) for x in (fingerprints, landmarks, whitening)),
    )

    theirs = lax.ppermute(other, "core", [(0, 1), (1, 0)])
    both = pl.pallas_call(
        add_theirs,
        in_specs=[vmem] * 2,
        out_specs=vmem,
        out_shape=f32(rows, half),
        compiler_params=small,
        name="add_theirs",
    )(own, theirs)
    parts = lax.all_to_all(both, "chip", 0, 0, tiled=True)

    turned, squares = pl.pallas_call(
        sum_parts,
        in_specs=[vmem],
        out_specs=[vmem] * 2,
        out_shape=[f32(half, 128), f32(8, 128)],
        compiler_params=small,
        name="sum_parts",
    )(parts.reshape(chips, owned, half))
    their_squares = lax.ppermute(squares, "core", [(0, 1), (1, 0)])
    blocks = pl.pallas_call(
        lay_out,
        in_specs=[vmem] * 2,
        out_specs=vmem,
        out_shape=f32(lines, chips, 128),
        compiler_params=small,
        name="lay_out",
    )(turned, pltpu.with_memory_space_constraint(memberships.reshape(-1, 128), pltpu.HBM))
    blocks = pl.pallas_call(
        functools.partial(normalise, feat=feat),
        in_specs=[vmem] * 3,
        out_specs=vmem,
        out_shape=f32(sources * lines, 128),
        compiler_params=small,
        name="normalise",
    )(blocks, squares, their_squares)
    blocks = lax.all_to_all(
        blocks.reshape(sources, 1, lines * 128), ("row", "chip"), 0, 0, tiled=True
    ).reshape(-1, 128)

    out = pl.pallas_call(
        centroid_update,
        in_specs=[vmem],
        out_specs=vmem,
        out_shape=f32(feat // (chips * cores), 4096 // n_row),
        scratch_shapes=[pltpu.VMEM((512, 128), jnp.float32)],
        compiler_params=small,
        name="centroid_update",
    )(blocks)
    return out.T


def solution(mesh):
    lm = ("chip", "core")
    inner = Mesh(mesh.devices.reshape(mesh.shape["row"], -1, 2), ("row",) + lm)
    in_specs = (P("row", None), P(lm, None), P(lm, None), P("row"))
    out_specs = P("row", lm)
    return jax.shard_map(
        on_device, mesh=inner, in_specs=in_specs, out_specs=out_specs, check_vma=False
    )
```

time: 63 us -> 58.9 us (0.935)
  blocking collectives: 0 us -> 42 us
  waiting for transfers between devices: 29.1 us -> 1.57 us
  starting transfers between devices: 21 us -> 5.49 us
  Pallas kernels: 11.4 us -> 9.57 us
  local copies, waits for them, and re-layouts: 1.04 us -> 0 us
    all_to_all x0 -> x2, blocking collectives: none -> 42 us  [the longest x1 26.9 us: on_device(): lax.all_to_all(blocks.reshape(sources, 1, lines * 128), ('row', 'chip'),...]
    all_to_all x2 -> x0, waiting for transfers between devices: 27.4 us -> none  [the longest x1 17.1 us: on_device(): lax.all_to_all(blocks.reshape(n_row * n_lm, 1, 3 * 128), ('row', 'chip',...]
    all_to_all x2 -> x0, starting transfers between devices: 17.7 us -> none  [the longest x1 12.7 us: on_device(): lax.all_to_all(blocks.reshape(n_row * n_lm, 1, 3 * 128), ('row', 'chip',...]
    ppermute x0 -> x1, starting transfers between devices: none -> 2.17 us  [on_device(): their_squares = lax.ppermute(squares, 'core', [(0, 1), (1, 0)])]
    pallas_call x3 -> x5, Pallas kernels: 10.6 us -> 9.52 us  [the longest x1 6.85 us: on_device(): pl.pallas_call(partial_features, in_specs=[hbm] * 3, out_specs=[vmem, vme...]
    unnamed x4 -> x0, local copies, waits for them, and re-layouts: 1.04 us -> none
    pallas_call x1, Pallas kernels: 0.84 us -> 0.05 us  [on_device(): pl.pallas_call(add_theirs, in_specs=[vmem] * 2, out_specs=vmem, out_shape...]
  transfers between devices with their start and end apart: 3 -> 2, of which waited for: 3 -> 1; matrix products, arithmetic and copies ran while one was open for 0% -> 0% of each run, Pallas kernels for 0% -> 1%
where the time goes in v3:
time: 58.9 us; the launch traced here: 58.7 us
  blocking collectives  42 us (71%)
  Pallas kernels  9.57 us (16%)
  starting transfers between devices  5.49 us (9%)
  waiting for transfers between devices  1.57 us (3%)
    all_to_all x1, blocking collectives, on_device(): lax.all_to_all(blocks.reshape(sources, 1, lines * 128), ('row', 'chip'),...  26.9 us
    all_to_all x1, blocking collectives, on_device(): parts = lax.all_to_all(both, 'chip', 0, 0, tiled=True)  15.2 us
    pallas_call x1, Pallas kernels, on_device(): pl.pallas_call(partial_features, in_specs=[hbm] * 3, out_specs=[vmem, vme...  6.85 us
    ppermute x1, starting transfers between devices, on_device(): theirs = lax.ppermute(other, 'core', [(0, 1), (1, 0)])  3.32 us
    ppermute x1, starting transfers between devices, on_device(): their_squares = lax.ppermute(squares, 'core', [(0, 1), (1, 0)])  2.17 us
    pallas_call x1, Pallas kernels, on_device(): pl.pallas_call(centroid_update, in_specs=[vmem], out_specs=vmem, out_shap...  1.63 us
    ppermute x1, waiting for transfers between devices, on_device(): theirs = lax.ppermute(other, 'core', [(0, 1), (1, 0)])  1.54 us
  transfers between devices with their start and end apart: 2, of which 1 were waited for; matrix products, arithmetic and copies ran while one was open for 0% of the time, Pallas kernels for 1%

profile of v3, /device:TPU:1, one launch (start us, length us, event | category | flops | bytes accessed | tf_op | source)
XLA Modules:
  0.0 58.7 jit_solution(3424217230716114113)
XLA Ops:
  0.0 6.8 %partial_features.1 = (f32[512,256]{1,0:T(8,128)S(1)}, f32[512,256]{1,0:T(8,128)S(1)}) custom-call(s32[512,2048]{1,0:T(8,128)} %fp.1, s32[512,2048]{1,0:T(8,128)} %lm.1, bf16[512,512]{1,0:T(8,128)(2,1)} %w.1), custom_call_target="tpu_custom_call" | custom-call | tf_op jit(solution)/shard_map/partial_features/pallas_call | solution.py:166
  6.9 3.3 %collective-permute-start = (f32[512,256]{1,0:T(8,128)S(1)}, f32[512,256]{1,0:T(8,128)S(1)}, u32[]{:S(2)}, u32[]{:S(2)}) collective-permute-start(f32[512,256]{1,0:T(8,128)S(1)} %get-tuple-element.10), channel_id=1, source_target_pairs={{0,1},{1,0},{2,3},{3,2},{4,5},{5,4},{6,7},{7,6},{8,9},{9,8},{10,11... | collective-permute-start | bytes 1572872 | tf_op jit(solution)/shard_map/ppermute | solution.py:188
  10.2 1.5 %collective-permute-done.theirs = f32[512,256]{1,0:T(8,128)S(1)} collective-permute-done((f32[512,256]{1,0:T(8,128)S(1)}, f32[512,256]{1,0:T(8,128)S(1)}, u32[]{:S(2)}, u32[]{:S(2)}) %collective-permute-start) | collective-permute-done | bytes 524320 | tf_op jit(solution)/shard_map/ppermute | solution.py:188
  11.7 0.1 add_theirs.1
  11.8 15.2 %all_to_all.14.parts = f32[16,32,256]{2,1,0:T(8,128)S(1)} all-to-all(f32[16,32,256]{2,1,0:T(8,128)S(1)} %bitcast.5), channel_id=1, replica_groups=mesh['row'=8,'chip'=16,'core'=2] {'chip'}, dimensions={0} | all-to-all | bytes 1048576 | tf_op jit(solution)/shard_map/all_to_all | solution.py:197
  27.0 0.1 sum_parts.1
  27.1 2.2 %collective-permute-start.1 = (f32[8,128]{1,0:T(8,128)S(1)}, f32[8,128]{1,0:T(8,128)S(1)}, u32[]{:S(2)}, u32[]{:S(2)}) collective-permute-start(f32[8,128]{1,0:T(8,128)S(1)} %get-tuple-element.12.mine), channel_id=1, source_target_pairs={{0,1},{1,0},{2,3},{3,2},{4,5},{5,4},{6,7},{7,6},{8,9},{9,8},{10,11... | collective-permute-start | bytes 12296 | tf_op jit(solution)/shard_map/ppermute | solution.py:207
  29.3 0.8 %lay_out.1.lines = f32[5,16,128]{2,1,0:T(8,128)S(1)} custom-call(f32[256,128]{1,0:T(8,128)S(1)} %get-tuple-element.11.turned, s32[4,128]{1,0:T(4,128)} %bitcast.8), custom_call_target="tpu_custom_call" | custom-call | tf_op jit(solution)/shard_map/lay_out/pallas_call | solution.py:208
  30.1 0.0 collective-permute-done.1.theirs
  30.1 0.1 normalise.1
  30.2 26.9 %all_to_all.15 = f32[128,1,640]{2,1,0:T(1,128)S(1)} all-to-all(f32[128,1,640]{2,1,0:T(1,128)S(1)} %bitcast.6), channel_id=1, replica_groups=mesh['row'=8,'chip'=16,'core'=2] {'row','chip'}, dimensions={0} | all-to-all | bytes 655360 | tf_op jit(solution)/shard_map/all_to_all | solution.py:224
  57.1 1.6 %centroid_update.1 = f32[16,512]{1,0:T(8,128)} custom-call(f32[640,128]{1,0:T(8,128)S(1)} %bitcast.7), custom_call_target="tpu_custom_call" | custom-call | tf_op jit(solution)/shard_map/centroid_update/pallas_call | solution.py:228
Async XLA Ops:
  6.9 4.9 %collective-permute-start = (f32[512,256]{1,0:T(8,128)S(1)}, f32[512,256]{1,0:T(8,128)S(1)}, u32[]{:S(2)}, u32[]{:S(2)}) collective-permute-start(f32[512,256]{1,0:T(8,128)S(1)} %get-tuple-element.10), channel_id=1, source_target_pairs={{0,1},{1,0},{2,3},{3,2},{4,5},{5,4},{6,7},{7,6},{8,9},{9,8},{10,11... | collective-permute-start | bytes 1572872 | tf_op jit(solution)/shard_map/ppermute | solution.py:188
  27.1 3.0 %collective-permute-start.1 = (f32[8,128]{1,0:T(8,128)S(1)}, f32[8,128]{1,0:T(8,128)S(1)}, u32[]{:S(2)}, u32[]{:S(2)}) collective-permute-start(f32[8,128]{1,0:T(8,128)S(1)} %get-tuple-element.12.mine), channel_id=1, source_target_pairs={{0,1},{1,0},{2,3},{3,2},{4,5},{5,4},{6,7},{7,6},{8,9},{9,8},{10,11... | collective-permute-start | bytes 12296 | tf_op jit(solution)/shard_map/ppermute | solution.py:207

commit v4 on v3

--- a/solution.py
+++ b/solution.py
@@ -5,12 +5,11 @@
 from jax import lax
 from jax.experimental import pallas as pl
 from jax.experimental.pallas import tpu as pltpu
-from jax.sharding import Mesh
 from jax.sharding import PartitionSpec as P
 
 LEVELS = 7
 F8 = jnp.float8_e4m3fn
-CHUNKS = (128, 128, 256, 512, 512, 512)
+CHUNKS = (256, 512, 512, 512, 256)
 MIB = 1 << 20
 
 
@@ -40,8 +39,8 @@
     half = feat // 2
     column = lax.broadcasted_iota(jnp.int32, (feat, half), 0)
     place = lax.broadcasted_iota(jnp.int32, (feat, half), 1)
-    place = 2 * (place - place % 16) + place % 16
-    this = lax.axis_index("core")
+    place = feat - 32 - 2 * (place - place % 16) + place % 16
+    this = lax.axis_index("lm") % 2
     w_copy.wait()
     for part, core in enumerate((1 - this, this)):
         pick = jnp.where(column == place + 16 * core, 1.0, 0.0).astype(jnp.bfloat16)
@@ -78,13 +77,10 @@
             shared[...] += part
         if i + 1 < len(CHUNKS):
             convert(i + 1)
-    step = 256
-    for at in range(0, shared.shape[0], step):
-        rows = pl.ds(at, step)
-        s = shared[rows, :]
-        kernel = (s / (row_total[rows, :] + land_total[...] - s)).astype(jnp.bfloat16)
-        raw = jnp.dot(kernel, turned_w[...], preferred_element_type=jnp.float32)
-        other[rows, :], own[rows, :] = raw[:, :half], raw[:, half:]
+    s = shared[...]
+    kernel = (s / (row_total[...] + land_total[...] - s)).astype(jnp.bfloat16)
+    raw = jnp.dot(kernel, turned_w[...], preferred_element_type=jnp.float32)
+    other[...], own[...] = raw[:, :half], raw[:, half:]
 
 
 def add_theirs(own, theirs, both):
@@ -108,7 +104,7 @@
         lines[h] = jnp.concatenate(
             [turned[pl.ds(4 * h + f, owners, stride=16), :][:, :rows] for f in range(4)], 1
         )
-    chip = lax.axis_index("chip")
+    chip = owners - 1 - lax.axis_index("lm") // 2
     line = member[pl.ds(chip // 4, 1), :].astype(jnp.float32)
     line = pltpu.roll(line, 128 - rows * (chip % 4), axis=1)
     lines[count] = jnp.broadcast_to(line, (owners, 128))
@@ -152,10 +148,15 @@
 def on_device(fingerprints, landmarks, whitening, memberships):
     rows, width = fingerprints.shape
     lands, feat = whitening.shape
-    n_row, chips, cores = (lax.axis_size(a) for a in ("row", "chip", "core"))
+    n_row, n_lm = lax.axis_size("row"), lax.axis_size("lm")
+    cores = 2
+    chips = n_lm // cores
     half = feat // cores
     owned = rows // chips
     sources, lines = n_row * chips, 5
+    swap = [(i, i ^ 1) for i in range(n_lm)]
+    plane = [[i for i in reversed(range(n_lm)) if i % cores == k] for k in range(cores)]
+    whole = [[i for i in reversed(range(n_row * n_lm)) if i % cores == k] for k in range(cores)]
     hbm, vmem = (pl.BlockSpec(memory_space=m) for m in (pltpu.HBM, pltpu.VMEM))
     factor = pltpu.VMEM((rows, LEVELS * max(CHUNKS)), F8)
     small = pltpu.CompilerParams(vmem_limit_bytes=12 * MIB)
@@ -185,7 +186,7 @@
         *(pltpu.with_memory_space_constraint(x, pltpu.HBM) for x in (fingerprints, landmarks, whitening)),
     )
 
-    theirs = lax.ppermute(other, "core", [(0, 1), (1, 0)])
+    theirs = lax.ppermute(other, "lm", swap)
     both = pl.pallas_call(
         add_theirs,
         in_specs=[vmem] * 2,
@@ -194,7 +195,7 @@
         compiler_params=small,
         name="add_theirs",
     )(own, theirs)
-    parts = lax.all_to_all(both, "chip", 0, 0, tiled=True)
+    parts = lax.all_to_all(both, "lm", 0, 0, tiled=True, axis_index_groups=plane)
 
     turned, squares = pl.pallas_call(
         sum_parts,
@@ -204,7 +205,7 @@
         compiler_params=small,
         name="sum_parts",
     )(parts.reshape(chips, owned, half))
-    their_squares = lax.ppermute(squares, "core", [(0, 1), (1, 0)])
+    their_squares = lax.ppermute(squares, "lm", swap)
     blocks = pl.pallas_call(
         lay_out,
         in_specs=[vmem] * 2,
@@ -222,7 +223,7 @@
         name="normalise",
     )(blocks, squares, their_squares)
     blocks = lax.all_to_all(
-        blocks.reshape(sources, 1, lines * 128), ("row", "chip"), 0, 0, tiled=True
+        blocks.reshape(sources, 1, lines * 128), ("row", "lm"), 0, 0, tiled=True, axis_index_groups=whole
     ).reshape(-1, 128)
 
     out = pl.pallas_call(
@@ -238,10 +239,8 @@
 
 
 def solution(mesh):
-    lm = ("chip", "core")
-    inner = Mesh(mesh.devices.reshape(mesh.shape["row"], -1, 2), ("row",) + lm)
-    in_specs = (P("row", None), P(lm, None), P(lm, None), P("row"))
-    out_specs = P("row", lm)
+    in_specs = (P("row", None), P("lm", None), P("lm", None), P("row"))
+    out_specs = P("row", "lm")
     return jax.shard_map(
-        on_device, mesh=inner, in_specs=in_specs, out_specs=out_specs, check_vma=False
+        on_device, mesh=mesh, in_specs=in_specs, out_specs=out_specs, check_vma=False
     )

time: 58.9 us -> 54.9 us (0.932); the launches traced: 58.7 us -> 53.9 us
  blocking collectives: 42 us -> 37.3 us
    all_to_all x2, blocking collectives: 42 us -> 37.3 us  [the longest x1 24.8 us: on_device(): lax.all_to_all(blocks.reshape(sources, 1, lines * 128), ('row', 'lm'), 0,...]
where the time goes in v4:
time: 54.9 us; the launch traced here: 53.9 us
  blocking collectives  37.3 us (68%)
  Pallas kernels  9.39 us (17%)
  starting transfers between devices  5.62 us (10%)
  waiting for transfers between devices  1.57 us (3%)
    all_to_all x1, blocking collectives, on_device(): lax.all_to_all(blocks.reshape(sources, 1, lines * 128), ('row', 'lm'), 0,...  24.8 us
    all_to_all x1, blocking collectives, on_device(): lax.all_to_all(both, 'lm', 0, 0, tiled=True, axis_index_groups=plane)  12.5 us
    pallas_call x1, Pallas kernels, on_device(): pl.pallas_call(partial_features, in_specs=[hbm] * 3, out_specs=[vmem, vme...  6.67 us
    ppermute x1, starting transfers between devices, on_device(): theirs = lax.ppermute(other, 'lm', swap)  3.33 us
    ppermute x1, starting transfers between devices, on_device(): their_squares = lax.ppermute(squares, 'lm', swap)  2.29 us
    pallas_call x1, Pallas kernels, on_device(): pl.pallas_call(centroid_update, in_specs=[vmem], out_specs=vmem, out_shap...  1.63 us
    ppermute x1, waiting for transfers between devices, on_device(): theirs = lax.ppermute(other, 'lm', swap)  1.54 us
  transfers between devices with their start and end apart: 2, of which 1 were waited for; matrix products, arithmetic and copies ran while one was open for 0% of the time, Pallas kernels for 1%

profile of v4, /device:TPU:1, one launch (start us, length us, event | category | flops | bytes accessed | tf_op | source)
XLA Modules:
  0.0 53.9 jit_solution(1626968784825045271)
XLA Ops:
  0.0 6.7 %partial_features.1 = (f32[512,256]{1,0:T(8,128)S(1)}, f32[512,256]{1,0:T(8,128)S(1)}) custom-call(s32[512,2048]{1,0:T(8,128)} %fp.1, s32[512,2048]{1,0:T(8,128)} %lm.1, bf16[512,512]{1,0:T(8,128)(2,1)} %w.1), custom_call_target="tpu_custom_call" | custom-call | tf_op jit(solution)/shard_map/partial_features/pallas_call | solution.py:167
  6.7 3.3 %collective-permute-start = (f32[512,256]{1,0:T(8,128)S(1)}, f32[512,256]{1,0:T(8,128)S(1)}, u32[]{:S(2)}, u32[]{:S(2)}) collective-permute-start(f32[512,256]{1,0:T(8,128)S(1)} %get-tuple-element.10), channel_id=1, source_target_pairs={{0,1},{1,0},{2,3},{3,2},{4,5},{5,4},{6,7},{7,6},{8,9},{9,8},{10,11... | collective-permute-start | bytes 1572872 | tf_op jit(solution)/shard_map/ppermute | solution.py:189
  10.0 1.5 %collective-permute-done.theirs = f32[512,256]{1,0:T(8,128)S(1)} collective-permute-done((f32[512,256]{1,0:T(8,128)S(1)}, f32[512,256]{1,0:T(8,128)S(1)}, u32[]{:S(2)}, u32[]{:S(2)}) %collective-permute-start) | collective-permute-done | bytes 524320 | tf_op jit(solution)/shard_map/ppermute | solution.py:189
  11.5 0.1 add_theirs.1
  11.6 12.5 %all_to_all.14.parts = f32[16,32,256]{2,1,0:T(8,128)S(1)} all-to-all(f32[16,32,256]{2,1,0:T(8,128)S(1)} %bitcast.5), channel_id=1, replica_groups={{30,28,26,24,22,20,18,16,14,12,10,8,6,4,2,0},{31,29,27,25,23,21,19,17,1..., dimensions={0} | all-to-all | bytes 1048576 | tf_op jit(solution)/shard_map/all_to_all | solution.py:198
  24.1 0.1 sum_parts.1
  24.3 2.3 %collective-permute-start.1 = (f32[8,128]{1,0:T(8,128)S(1)}, f32[8,128]{1,0:T(8,128)S(1)}, u32[]{:S(2)}, u32[]{:S(2)}) collective-permute-start(f32[8,128]{1,0:T(8,128)S(1)} %get-tuple-element.12.mine), channel_id=1, source_target_pairs={{0,1},{1,0},{2,3},{3,2},{4,5},{5,4},{6,7},{7,6},{8,9},{9,8},{10,11... | collective-permute-start | bytes 12296 | tf_op jit(solution)/shard_map/ppermute | solution.py:208
  26.5 0.8 %lay_out.1.lines = f32[5,16,128]{2,1,0:T(8,128)S(1)} custom-call(f32[256,128]{1,0:T(8,128)S(1)} %get-tuple-element.11.turned, s32[4,128]{1,0:T(4,128)} %bitcast.8), custom_call_target="tpu_custom_call" | custom-call | tf_op jit(solution)/shard_map/lay_out/pallas_call | solution.py:209
  27.3 0.0 collective-permute-done.1.theirs
  27.4 0.1 normalise.1
  27.5 24.8 %all_to_all.15 = f32[128,1,640]{2,1,0:T(1,128)S(1)} all-to-all(f32[128,1,640]{2,1,0:T(1,128)S(1)} %bitcast.6), channel_id=1, replica_groups={{254,252,250,248,246,244,242,240,238,236,234,232,230,228,226,224,222,22..., dimensions={0} | all-to-all | bytes 655360 | tf_op jit(solution)/shard_map/all_to_all | solution.py:225
  52.2 1.6 %centroid_update.1 = f32[16,512]{1,0:T(8,128)} custom-call(f32[640,128]{1,0:T(8,128)S(1)} %bitcast.7), custom_call_target="tpu_custom_call" | custom-call | tf_op jit(solution)/shard_map/centroid_update/pallas_call | solution.py:229
Async XLA Ops:
  6.7 4.9 %collective-permute-start = (f32[512,256]{1,0:T(8,128)S(1)}, f32[512,256]{1,0:T(8,128)S(1)}, u32[]{:S(2)}, u32[]{:S(2)}) collective-permute-start(f32[512,256]{1,0:T(8,128)S(1)} %get-tuple-element.10), channel_id=1, source_target_pairs={{0,1},{1,0},{2,3},{3,2},{4,5},{5,4},{6,7},{7,6},{8,9},{9,8},{10,11... | collective-permute-start | bytes 1572872 | tf_op jit(solution)/shard_map/ppermute | solution.py:189
  24.3 3.1 %collective-permute-start.1 = (f32[8,128]{1,0:T(8,128)S(1)}, f32[8,128]{1,0:T(8,128)S(1)}, u32[]{:S(2)}, u32[]{:S(2)}) collective-permute-start(f32[8,128]{1,0:T(8,128)S(1)} %get-tuple-element.12.mine), channel_id=1, source_target_pairs={{0,1},{1,0},{2,3},{3,2},{4,5},{5,4},{6,7},{7,6},{8,9},{9,8},{10,11... | collective-permute-start | bytes 12296 | tf_op jit(solution)/shard_map/ppermute | solution.py:208

commit v5 on v4

--- a/solution.py
+++ b/solution.py
@@ -156,7 +156,8 @@
     sources, lines = n_row * chips, 5
     swap = [(i, i ^ 1) for i in range(n_lm)]
     plane = [[i for i in reversed(range(n_lm)) if i % cores == k] for k in range(cores)]
-    whole = [[i for i in reversed(range(n_row * n_lm)) if i % cores == k] for k in range(cores)]
+    order = [z for pair in zip(reversed(range(n_row // 2, n_row)), reversed(range(n_row // 2))) for z in pair]
+    whole = [[z * n_lm + i for z in order for i in plane[k]] for k in range(cores)]
     hbm, vmem = (pl.BlockSpec(memory_space=m) for m in (pltpu.HBM, pltpu.VMEM))
     factor = pltpu.VMEM((rows, LEVELS * max(CHUNKS)), F8)
     small = pltpu.CompilerParams(vmem_limit_bytes=12 * MIB)

time: 54.9 us -> 53.6 us (0.976); the launches traced: 53.9 us -> 53.1 us
  blocking collectives: 37.3 us -> 36.5 us
    all_to_all x1, blocking collectives: 24.8 us -> 24 us  [on_device(): lax.all_to_all(blocks.reshape(sources, 1, lines * 128), ('row', 'lm'), 0,...]
where the time goes in v5:
time: 53.6 us; the launch traced here: 53.1 us
  blocking collectives  36.5 us (68%)
  Pallas kernels  9.39 us (18%)
  starting transfers between devices  5.62 us (10%)
  waiting for transfers between devices  1.57 us (3%)
    all_to_all x1, blocking collectives, on_device(): lax.all_to_all(blocks.reshape(sources, 1, lines * 128), ('row', 'lm'), 0,...  24 us
    all_to_all x1, blocking collectives, on_device(): lax.all_to_all(both, 'lm', 0, 0, tiled=True, axis_index_groups=plane)  12.5 us
    pallas_call x1, Pallas kernels, on_device(): pl.pallas_call(partial_features, in_specs=[hbm] * 3, out_specs=[vmem, vme...  6.67 us
    ppermute x1, starting transfers between devices, on_device(): theirs = lax.ppermute(other, 'lm', swap)  3.33 us
    ppermute x1, starting transfers between devices, on_device(): their_squares = lax.ppermute(squares, 'lm', swap)  2.29 us
    pallas_call x1, Pallas kernels, on_device(): pl.pallas_call(centroid_update, in_specs=[vmem], out_specs=vmem, out_shap...  1.63 us
    ppermute x1, waiting for transfers between devices, on_device(): theirs = lax.ppermute(other, 'lm', swap)  1.54 us
  transfers between devices with their start and end apart: 2, of which 1 were waited for; matrix products, arithmetic and copies ran while one was open for 0% of the time, Pallas kernels for 1%

profile of v5, /device:TPU:1, one launch (start us, length us, event | category | flops | bytes accessed | tf_op | source)
XLA Modules:
  0.0 53.1 jit_solution(10326173770745308320)
XLA Ops:
  0.0 6.7 %partial_features.1 = (f32[512,256]{1,0:T(8,128)S(1)}, f32[512,256]{1,0:T(8,128)S(1)}) custom-call(s32[512,2048]{1,0:T(8,128)} %fp.1, s32[512,2048]{1,0:T(8,128)} %lm.1, bf16[512,512]{1,0:T(8,128)(2,1)} %w.1), custom_call_target="tpu_custom_call" | custom-call | tf_op jit(solution)/shard_map/partial_features/pallas_call | solution.py:168
  6.7 3.3 %collective-permute-start = (f32[512,256]{1,0:T(8,128)S(1)}, f32[512,256]{1,0:T(8,128)S(1)}, u32[]{:S(2)}, u32[]{:S(2)}) collective-permute-start(f32[512,256]{1,0:T(8,128)S(1)} %get-tuple-element.10), channel_id=1, source_target_pairs={{0,1},{1,0},{2,3},{3,2},{4,5},{5,4},{6,7},{7,6},{8,9},{9,8},{10,11... | collective-permute-start | bytes 1572872 | tf_op jit(solution)/shard_map/ppermute | solution.py:190
  10.0 1.5 %collective-permute-done.theirs = f32[512,256]{1,0:T(8,128)S(1)} collective-permute-done((f32[512,256]{1,0:T(8,128)S(1)}, f32[512,256]{1,0:T(8,128)S(1)}, u32[]{:S(2)}, u32[]{:S(2)}) %collective-permute-start) | collective-permute-done | bytes 524320 | tf_op jit(solution)/shard_map/ppermute | solution.py:190
  11.5 0.1 add_theirs.1
  11.6 12.5 %all_to_all.14.parts = f32[16,32,256]{2,1,0:T(8,128)S(1)} all-to-all(f32[16,32,256]{2,1,0:T(8,128)S(1)} %bitcast.5), channel_id=1, replica_groups={{30,28,26,24,22,20,18,16,14,12,10,8,6,4,2,0},{31,29,27,25,23,21,19,17,1..., dimensions={0} | all-to-all | bytes 1048576 | tf_op jit(solution)/shard_map/all_to_all | solution.py:199
  24.1 0.1 sum_parts.1
  24.3 2.3 %collective-permute-start.1 = (f32[8,128]{1,0:T(8,128)S(1)}, f32[8,128]{1,0:T(8,128)S(1)}, u32[]{:S(2)}, u32[]{:S(2)}) collective-permute-start(f32[8,128]{1,0:T(8,128)S(1)} %get-tuple-element.12.mine), channel_id=1, source_target_pairs={{0,1},{1,0},{2,3},{3,2},{4,5},{5,4},{6,7},{7,6},{8,9},{9,8},{10,11... | collective-permute-start | bytes 12296 | tf_op jit(solution)/shard_map/ppermute | solution.py:209
  26.5 0.8 %lay_out.1.lines = f32[5,16,128]{2,1,0:T(8,128)S(1)} custom-call(f32[256,128]{1,0:T(8,128)S(1)} %get-tuple-element.11.turned, s32[4,128]{1,0:T(4,128)} %bitcast.8), custom_call_target="tpu_custom_call" | custom-call | tf_op jit(solution)/shard_map/lay_out/pallas_call | solution.py:210
  27.3 0.0 collective-permute-done.1.theirs
  27.4 0.1 normalise.1
  27.5 24.0 %all_to_all.15 = f32[128,1,640]{2,1,0:T(1,128)S(1)} all-to-all(f32[128,1,640]{2,1,0:T(1,128)S(1)} %bitcast.6), channel_id=1, replica_groups={{254,252,250,248,246,244,242,240,238,236,234,232,230,228,226,224,126,12..., dimensions={0} | all-to-all | bytes 655360 | tf_op jit(solution)/shard_map/all_to_all | solution.py:226
  51.5 1.6 %centroid_update.1 = f32[16,512]{1,0:T(8,128)} custom-call(f32[640,128]{1,0:T(8,128)S(1)} %bitcast.7), custom_call_target="tpu_custom_call" | custom-call | tf_op jit(solution)/shard_map/centroid_update/pallas_call | solution.py:230
Async XLA Ops:
  6.7 4.9 %collective-permute-start = (f32[512,256]{1,0:T(8,128)S(1)}, f32[512,256]{1,0:T(8,128)S(1)}, u32[]{:S(2)}, u32[]{:S(2)}) collective-permute-start(f32[512,256]{1,0:T(8,128)S(1)} %get-tuple-element.10), channel_id=1, source_target_pairs={{0,1},{1,0},{2,3},{3,2},{4,5},{5,4},{6,7},{7,6},{8,9},{9,8},{10,11... | collective-permute-start | bytes 1572872 | tf_op jit(solution)/shard_map/ppermute | solution.py:190
  24.3 3.1 %collective-permute-start.1 = (f32[8,128]{1,0:T(8,128)S(1)}, f32[8,128]{1,0:T(8,128)S(1)}, u32[]{:S(2)}, u32[]{:S(2)}) collective-permute-start(f32[8,128]{1,0:T(8,128)S(1)} %get-tuple-element.12.mine), channel_id=1, source_target_pairs={{0,1},{1,0},{2,3},{3,2},{4,5},{5,4},{6,7},{7,6},{8,9},{9,8},{10,11... | collective-permute-start | bytes 12296 | tf_op jit(solution)/shard_map/ppermute | solution.py:209

commit v6 on v5

--- a/solution.py
+++ b/solution.py
@@ -104,7 +104,8 @@
         lines[h] = jnp.concatenate(
             [turned[pl.ds(4 * h + f, owners, stride=16), :][:, :rows] for f in range(4)], 1
         )
-    chip = owners - 1 - lax.axis_index("lm") // 2
+    back = owners - 1 - lax.axis_index("lm") // 2
+    chip = 2 * (back % (owners // 2)) + back // (owners // 2)
     line = member[pl.ds(chip // 4, 1), :].astype(jnp.float32)
     line = pltpu.roll(line, 128 - rows * (chip % 4), axis=1)
     lines[count] = jnp.broadcast_to(line, (owners, 128))
@@ -156,6 +157,7 @@
     sources, lines = n_row * chips, 5
     swap = [(i, i ^ 1) for i in range(n_lm)]
     plane = [[i for i in reversed(range(n_lm)) if i % cores == k] for k in range(cores)]
+    turns = [[p[i // 2 + (i % 2) * (chips // 2)] for i in range(chips)] for p in plane]
     order = [z for pair in zip(reversed(range(n_row // 2, n_row)), reversed(range(n_row // 2))) for z in pair]
     whole = [[z * n_lm + i for z in order for i in plane[k]] for k in range(cores)]
     hbm, vmem = (pl.BlockSpec(memory_space=m) for m in (pltpu.HBM, pltpu.VMEM))
@@ -196,7 +198,7 @@
         compiler_params=small,
         name="add_theirs",
     )(own, theirs)
-    parts = lax.all_to_all(both, "lm", 0, 0, tiled=True, axis_index_groups=plane)
+    parts = lax.all_to_all(both, "lm", 0, 0, tiled=True, axis_index_groups=turns)
 
     turned, squares = pl.pallas_call(
         sum_parts,

time: 53.6 us -> 53.3 us (level)
    all_to_all x1, blocking collectives: 24 us -> 23.1 us  [on_device(): lax.all_to_all(blocks.reshape(sources, 1, lines * 128), ('row', 'lm'), 0,...]
    all_to_all x1, blocking collectives: 12.5 us -> 13.2 us  [on_device(): lax.all_to_all(both, 'lm', 0, 0, tiled=True, axis_index_groups=turns)]
  transfers between devices with their start and end apart: 2 -> 2, of which waited for: 1 -> 1; matrix products, arithmetic and copies ran while one was open for 0% -> 0% of each run, Pallas kernels for 1% -> 2%
where the time goes in v6:
time: 53.3 us; the launch traced here: 52.8 us
  blocking collectives  36.3 us (68%)
  Pallas kernels  9.39 us (18%)
  starting transfers between devices  5.51 us (10%)
  waiting for transfers between devices  1.57 us (3%)
    all_to_all x1, blocking collectives, on_device(): lax.all_to_all(blocks.reshape(sources, 1, lines * 128), ('row', 'lm'), 0,...  23.1 us
    all_to_all x1, blocking collectives, on_device(): lax.all_to_all(both, 'lm', 0, 0, tiled=True, axis_index_groups=turns)  13.2 us
    pallas_call x1, Pallas kernels, on_device(): pl.pallas_call(partial_features, in_specs=[hbm] * 3, out_specs=[vmem, vme...  6.67 us
    ppermute x1, starting transfers between devices, on_device(): theirs = lax.ppermute(other, 'lm', swap)  3.33 us
    ppermute x1, starting transfers between devices, on_device(): their_squares = lax.ppermute(squares, 'lm', swap)  2.18 us
    pallas_call x1, Pallas kernels, on_device(): pl.pallas_call(centroid_update, in_specs=[vmem], out_specs=vmem, out_shap...  1.63 us
    ppermute x1, waiting for transfers between devices, on_device(): theirs = lax.ppermute(other, 'lm', swap)  1.54 us
  transfers between devices with their start and end apart: 2, of which 1 were waited for; matrix products, arithmetic and copies ran while one was open for 0% of the time, Pallas kernels for 2%

profile of v6, /device:TPU:1, one launch (start us, length us, event | category | flops | bytes accessed | tf_op | source)
XLA Modules:
  0.0 52.8 jit_solution(10932529508777730660)
XLA Ops:
  0.0 6.7 %partial_features.1 = (f32[512,256]{1,0:T(8,128)S(1)}, f32[512,256]{1,0:T(8,128)S(1)}) custom-call(s32[512,2048]{1,0:T(8,128)} %fp.1, s32[512,2048]{1,0:T(8,128)} %lm.1, bf16[512,512]{1,0:T(8,128)(2,1)} %w.1), custom_call_target="tpu_custom_call" | custom-call | tf_op jit(solution)/shard_map/partial_features/pallas_call | solution.py:170
  6.7 3.3 %collective-permute-start = (f32[512,256]{1,0:T(8,128)S(1)}, f32[512,256]{1,0:T(8,128)S(1)}, u32[]{:S(2)}, u32[]{:S(2)}) collective-permute-start(f32[512,256]{1,0:T(8,128)S(1)} %get-tuple-element.10), channel_id=1, source_target_pairs={{0,1},{1,0},{2,3},{3,2},{4,5},{5,4},{6,7},{7,6},{8,9},{9,8},{10,11... | collective-permute-start | bytes 1572872 | tf_op jit(solution)/shard_map/ppermute | solution.py:192
  10.0 1.5 %collective-permute-done.theirs = f32[512,256]{1,0:T(8,128)S(1)} collective-permute-done((f32[512,256]{1,0:T(8,128)S(1)}, f32[512,256]{1,0:T(8,128)S(1)}, u32[]{:S(2)}, u32[]{:S(2)}) %collective-permute-start) | collective-permute-done | bytes 524320 | tf_op jit(solution)/shard_map/ppermute | solution.py:192
  11.5 0.1 add_theirs.1
  11.6 13.2 %all_to_all.14.parts = f32[16,32,256]{2,1,0:T(8,128)S(1)} all-to-all(f32[16,32,256]{2,1,0:T(8,128)S(1)} %bitcast.5), channel_id=1, replica_groups={{30,14,28,12,26,10,24,8,22,6,20,4,18,2,16,0},{31,15,29,13,27,11,25,9,23..., dimensions={0} | all-to-all | bytes 1048576 | tf_op jit(solution)/shard_map/all_to_all | solution.py:201
  24.8 0.1 sum_parts.1
  24.9 2.2 %collective-permute-start.1 = (f32[8,128]{1,0:T(8,128)S(1)}, f32[8,128]{1,0:T(8,128)S(1)}, u32[]{:S(2)}, u32[]{:S(2)}) collective-permute-start(f32[8,128]{1,0:T(8,128)S(1)} %get-tuple-element.12.mine), channel_id=1, source_target_pairs={{0,1},{1,0},{2,3},{3,2},{4,5},{5,4},{6,7},{7,6},{8,9},{9,8},{10,11... | collective-permute-start | bytes 12296 | tf_op jit(solution)/shard_map/ppermute | solution.py:211
  27.1 0.8 %lay_out.1.lines = f32[5,16,128]{2,1,0:T(8,128)S(1)} custom-call(f32[256,128]{1,0:T(8,128)S(1)} %get-tuple-element.11.turned, s32[4,128]{1,0:T(4,128)} %bitcast.8), custom_call_target="tpu_custom_call" | custom-call | tf_op jit(solution)/shard_map/lay_out/pallas_call | solution.py:212
  27.9 0.0 collective-permute-done.1.theirs
  27.9 0.1 normalise.1
  28.0 23.1 %all_to_all.15 = f32[128,1,640]{2,1,0:T(1,128)S(1)} all-to-all(f32[128,1,640]{2,1,0:T(1,128)S(1)} %bitcast.6), channel_id=1, replica_groups={{254,252,250,248,246,244,242,240,238,236,234,232,230,228,226,224,126,12..., dimensions={0} | all-to-all | bytes 655360 | tf_op jit(solution)/shard_map/all_to_all | solution.py:228
  51.1 1.6 %centroid_update.1 = f32[16,512]{1,0:T(8,128)} custom-call(f32[640,128]{1,0:T(8,128)S(1)} %bitcast.7), custom_call_target="tpu_custom_call" | custom-call | tf_op jit(solution)/shard_map/centroid_update/pallas_call | solution.py:232
Async XLA Ops:
  6.7 4.9 %collective-permute-start = (f32[512,256]{1,0:T(8,128)S(1)}, f32[512,256]{1,0:T(8,128)S(1)}, u32[]{:S(2)}, u32[]{:S(2)}) collective-permute-start(f32[512,256]{1,0:T(8,128)S(1)} %get-tuple-element.10), channel_id=1, source_target_pairs={{0,1},{1,0},{2,3},{3,2},{4,5},{5,4},{6,7},{7,6},{8,9},{9,8},{10,11... | collective-permute-start | bytes 1572872 | tf_op jit(solution)/shard_map/ppermute | solution.py:192
  24.9 3.0 %collective-permute-start.1 = (f32[8,128]{1,0:T(8,128)S(1)}, f32[8,128]{1,0:T(8,128)S(1)}, u32[]{:S(2)}, u32[]{:S(2)}) collective-permute-start(f32[8,128]{1,0:T(8,128)S(1)} %get-tuple-element.12.mine), channel_id=1, source_target_pairs={{0,1},{1,0},{2,3},{3,2},{4,5},{5,4},{6,7},{7,6},{8,9},{9,8},{10,11... | collective-permute-start | bytes 12296 | tf_op jit(solution)/shard_map/ppermute | solution.py:211

commit v7 on v6

--- a/solution.py
+++ b/solution.py
@@ -105,7 +105,7 @@
             [turned[pl.ds(4 * h + f, owners, stride=16), :][:, :rows] for f in range(4)], 1
         )
     back = owners - 1 - lax.axis_index("lm") // 2
-    chip = 2 * (back % (owners // 2)) + back // (owners // 2)
+    chip = 8 * (back % 2) + 4 * (back // 2 % 2) + 2 * (back // 4 % 2) + back // 8
     line = member[pl.ds(chip // 4, 1), :].astype(jnp.float32)
     line = pltpu.roll(line, 128 - rows * (chip % 4), axis=1)
     lines[count] = jnp.broadcast_to(line, (owners, 128))
@@ -157,7 +157,7 @@
     sources, lines = n_row * chips, 5
     swap = [(i, i ^ 1) for i in range(n_lm)]
     plane = [[i for i in reversed(range(n_lm)) if i % cores == k] for k in range(cores)]
-    turns = [[p[i // 2 + (i % 2) * (chips // 2)] for i in range(chips)] for p in plane]
+    turns = [[p[8 * (i % 2) + 4 * (i // 2 % 2) + 2 * (i // 4 % 2) + i // 8] for i in range(chips)] for p in plane]
     order = [z for pair in zip(reversed(range(n_row // 2, n_row)), reversed(range(n_row // 2))) for z in pair]
     whole = [[z * n_lm + i for z in order for i in plane[k]] for k in range(cores)]
     hbm, vmem = (pl.BlockSpec(memory_space=m) for m in (pltpu.HBM, pltpu.VMEM))

time: 53.3 us -> 53.6 us (level)
    all_to_all x1, blocking collectives: 23.1 us -> 24.1 us  [on_device(): lax.all_to_all(blocks.reshape(sources, 1, lines * 128), ('row', 'lm'), 0,...]
    all_to_all x1, blocking collectives: 13.2 us -> 12.6 us  [on_device(): lax.all_to_all(both, 'lm', 0, 0, tiled=True, axis_index_groups=turns)]
where the time goes in v7:
time: 53.6 us; the launch traced here: 53.1 us
  blocking collectives  36.7 us (68%)
  Pallas kernels  9.4 us (18%)
  starting transfers between devices  5.5 us (10%)
  waiting for transfers between devices  1.56 us (3%)
    all_to_all x1, blocking collectives, on_device(): lax.all_to_all(blocks.reshape(sources, 1, lines * 128), ('row', 'lm'), 0,...  24.1 us
    all_to_all x1, blocking collectives, on_device(): lax.all_to_all(both, 'lm', 0, 0, tiled=True, axis_index_groups=turns)  12.6 us
    pallas_call x1, Pallas kernels, on_device(): pl.pallas_call(partial_features, in_specs=[hbm] * 3, out_specs=[vmem, vme...  6.67 us
    ppermute x1, starting transfers between devices, on_device(): theirs = lax.ppermute(other, 'lm', swap)  3.33 us
    ppermute x1, starting transfers between devices, on_device(): their_squares = lax.ppermute(squares, 'lm', swap)  2.17 us
    pallas_call x1, Pallas kernels, on_device(): pl.pallas_call(centroid_update, in_specs=[vmem], out_specs=vmem, out_shap...  1.63 us
    ppermute x1, waiting for transfers between devices, on_device(): theirs = lax.ppermute(other, 'lm', swap)  1.54 us
  transfers between devices with their start and end apart: 2, of which 1 were waited for; matrix products, arithmetic and copies ran while one was open for 0% of the time, Pallas kernels for 2%

profile of v7, /device:TPU:1, one launch (start us, length us, event | category | flops | bytes accessed | tf_op | source)
XLA Modules:
  0.0 53.1 jit_solution(14382680613842642421)
XLA Ops:
  0.0 6.7 %partial_features.1 = (f32[512,256]{1,0:T(8,128)S(1)}, f32[512,256]{1,0:T(8,128)S(1)}) custom-call(s32[512,2048]{1,0:T(8,128)} %fp.1, s32[512,2048]{1,0:T(8,128)} %lm.1, bf16[512,512]{1,0:T(8,128)(2,1)} %w.1), custom_call_target="tpu_custom_call" | custom-call | tf_op jit(solution)/shard_map/partial_features/pallas_call | solution.py:170
  6.7 3.3 %collective-permute-start = (f32[512,256]{1,0:T(8,128)S(1)}, f32[512,256]{1,0:T(8,128)S(1)}, u32[]{:S(2)}, u32[]{:S(2)}) collective-permute-start(f32[512,256]{1,0:T(8,128)S(1)} %get-tuple-element.10), channel_id=1, source_target_pairs={{0,1},{1,0},{2,3},{3,2},{4,5},{5,4},{6,7},{7,6},{8,9},{9,8},{10,11... | collective-permute-start | bytes 1572872 | tf_op jit(solution)/shard_map/ppermute | solution.py:192
  10.0 1.5 %collective-permute-done.theirs = f32[512,256]{1,0:T(8,128)S(1)} collective-permute-done((f32[512,256]{1,0:T(8,128)S(1)}, f32[512,256]{1,0:T(8,128)S(1)}, u32[]{:S(2)}, u32[]{:S(2)}) %collective-permute-start) | collective-permute-done | bytes 524320 | tf_op jit(solution)/shard_map/ppermute | solution.py:192
  11.5 0.1 add_theirs.1
  11.6 12.6 %all_to_all.14.parts = f32[16,32,256]{2,1,0:T(8,128)S(1)} all-to-all(f32[16,32,256]{2,1,0:T(8,128)S(1)} %bitcast.5), channel_id=1, replica_groups={{30,14,22,6,26,10,18,2,28,12,20,4,24,8,16,0},{31,15,23,7,27,11,19,3,29,..., dimensions={0} | all-to-all | bytes 1048576 | tf_op jit(solution)/shard_map/all_to_all | solution.py:201
  24.2 0.1 sum_parts.1
  24.3 2.2 %collective-permute-start.1 = (f32[8,128]{1,0:T(8,128)S(1)}, f32[8,128]{1,0:T(8,128)S(1)}, u32[]{:S(2)}, u32[]{:S(2)}) collective-permute-start(f32[8,128]{1,0:T(8,128)S(1)} %get-tuple-element.12.mine), channel_id=1, source_target_pairs={{0,1},{1,0},{2,3},{3,2},{4,5},{5,4},{6,7},{7,6},{8,9},{9,8},{10,11... | collective-permute-start | bytes 12296 | tf_op jit(solution)/shard_map/ppermute | solution.py:211
  26.5 0.8 %lay_out.1.lines = f32[5,16,128]{2,1,0:T(8,128)S(1)} custom-call(f32[256,128]{1,0:T(8,128)S(1)} %get-tuple-element.11.turned, s32[4,128]{1,0:T(4,128)} %bitcast.8), custom_call_target="tpu_custom_call" | custom-call | tf_op jit(solution)/shard_map/lay_out/pallas_call | solution.py:212
  27.3 0.0 collective-permute-done.1.theirs
  27.3 0.1 normalise.1
  27.4 24.1 %all_to_all.15 = f32[128,1,640]{2,1,0:T(1,128)S(1)} all-to-all(f32[128,1,640]{2,1,0:T(1,128)S(1)} %bitcast.6), channel_id=1, replica_groups={{254,252,250,248,246,244,242,240,238,236,234,232,230,228,226,224,126,12..., dimensions={0} | all-to-all | bytes 655360 | tf_op jit(solution)/shard_map/all_to_all | solution.py:228
  51.5 1.6 %centroid_update.1 = f32[16,512]{1,0:T(8,128)} custom-call(f32[640,128]{1,0:T(8,128)S(1)} %bitcast.7), custom_call_target="tpu_custom_call" | custom-call | tf_op jit(solution)/shard_map/centroid_update/pallas_call | solution.py:232
Async XLA Ops:
  6.7 4.9 %collective-permute-start = (f32[512,256]{1,0:T(8,128)S(1)}, f32[512,256]{1,0:T(8,128)S(1)}, u32[]{:S(2)}, u32[]{:S(2)}) collective-permute-start(f32[512,256]{1,0:T(8,128)S(1)} %get-tuple-element.10), channel_id=1, source_target_pairs={{0,1},{1,0},{2,3},{3,2},{4,5},{5,4},{6,7},{7,6},{8,9},{9,8},{10,11... | collective-permute-start | bytes 1572872 | tf_op jit(solution)/shard_map/ppermute | solution.py:192
  24.3 3.0 %collective-permute-start.1 = (f32[8,128]{1,0:T(8,128)S(1)}, f32[8,128]{1,0:T(8,128)S(1)}, u32[]{:S(2)}, u32[]{:S(2)}) collective-permute-start(f32[8,128]{1,0:T(8,128)S(1)} %get-tuple-element.12.mine), channel_id=1, source_target_pairs={{0,1},{1,0},{2,3},{3,2},{4,5},{5,4},{6,7},{7,6},{8,9},{9,8},{10,11... | collective-permute-start | bytes 12296 | tf_op jit(solution)/shard_map/ppermute | solution.py:211
